TPU v7x, 512 devices: a whole 4x4x16 slice. The times are simulated.
512 devices in a mesh: rows: 64 (over z, y), cols: 8 (over x, core).
Axes of the slice: x: 4, y: 4, z: 16, core: 2. Of those that a mesh axis runs over, the one named last changes fastest.
Arguments:
- block_vector: float32 [524288, 128], P('rows'), may hold values from -6 to 6
- op_tiles: float32 [4096, 8, 128, 128], P('rows', 'cols')
- tile_cols: int32 [4096, 8], P('rows', 'cols'), may hold values from 0 to 4095, as said below
- live_counts: int32 [4096], P('rows'), may hold values from 1 to 8
Outputs:
- basis_block: float32 [524288, 128], P(('rows', 'cols'))
- r_factor: float32 [128, 128], replicated
Inputs may be any that keep to these rules, and one draw needn't show every extreme that they name: `tile_cols`: slot 0 of row block i names i itself. Every entry names a row block of the same index of rows as i, or of the index just before or after it.
All inputs are finite; a program needn't handle non-finite values.
Results may differ from a plain program's by a relative error of at most 0.0003.
Values sent between devices are 32-bit elements; how exact they have to be, the bound alone decides.
No kernel may reach another device: no remote copies, remote signals or barrier semaphores. Data moves between devices by JAX's collectives and lax.ppermute only.
A program may use at most 128 MiB of HBM per device.

v0:
```python
import jax
import jax.numpy as jnp
from jax import lax
from jax.sharding import PartitionSpec as P


def with_halo(cells, sides, width):
    for axis, dim in sides:
        count = lax.axis_size(axis)
        ends = count - 1
        head = lax.slice_in_dim(cells, 0, width, axis=dim)
        tail = lax.slice_in_dim(cells, cells.shape[dim] - width, cells.shape[dim], axis=dim)
        cells = jnp.concatenate(
            [
                lax.ppermute(tail, axis, [(i, (i + 1) % count) for i in range(ends)]),
                cells,
                lax.ppermute(head, axis, [((i + 1) % count, i) for i in range(ends)]),
            ],
            axis=dim,
        )
    return cells


def on_device(block_vector, op_tiles, tile_cols, live_counts):
    block_count, slot_count, tile_size, _ = op_tiles.shape
    vec_width = block_vector.shape[1]
    row_devices = lax.axis_size("rows")
    rows_here = block_count * tile_size
    extended = with_halo(block_vector, (("rows", 0),), rows_here)
    vec_blocks = extended.reshape(3 * block_count, tile_size, vec_width)
    first_block = lax.axis_index("rows") * block_count - block_count
    local_idx = tile_cols - first_block
    slot_ids = lax.axis_index("cols") * slot_count + jnp.arange(slot_count, dtype=jnp.int32)
    live_mask = (slot_ids[None, :] < live_counts[:, None]).astype(jnp.float32)
    picked = vec_blocks[local_idx] * live_mask[:, :, None, None]
    partial_value = jnp.einsum("jsab,jsbc->jac", op_tiles, picked, precision=lax.Precision.HIGHEST)
    partial_value = partial_value.reshape(rows_here, vec_width)
    part_rows = lax.psum_scatter(partial_value, "cols", scatter_dimension=0, tiled=True)
    local_gram = jnp.einsum("ra,rb->ab", part_rows, part_rows, precision=lax.Precision.HIGHEST)
    gram_matrix = lax.psum(local_gram, ("rows", "cols"))
    chol_lower = jnp.linalg.cholesky(gram_matrix)
    solved = jax.scipy.linalg.solve_triangular(chol_lower, part_rows.T, lower=True)
    root_nodes = jnp.sqrt(jnp.float32(rows_here * row_devices))
    return (solved.T * root_nodes, chol_lower.T / root_nodes)


def solution(mesh):
    in_specs = (P("rows", None), P("rows", "cols", None, None), P("rows", "cols"), P("rows"))
    out_specs = (P(("rows", "cols"), None), P())
    return jax.shard_map(
        on_device, mesh=mesh, in_specs=in_specs, out_specs=out_specs, check_vma=False
    )
```

profile of v0, /device:TPU:1, one launch (start us, length us, event | category | flops | bytes accessed | tf_op | source)
XLA Modules:
  0.0 666.9 jit_solution(15943087688216260176)
XLA Ops:
  7.2 0.0 reduce-scatter.2.cloned.1.call-start
  7.2 1.3 collective-permute-start.1
  8.5 6.6 collective-permute-start
  15.1 0.7 fusion.6
  15.8 0.7 compare_convert_fusion
  16.4 79.5 %collective-permute-done.1 = f32[8192,128]{1,0:T(8,128)} collective-permute-done((f32[8192,128]{1,0:T(8,128)}, f32[8192,128]{1,0:T(8,128)}, u32[]{:S(2)}, u32[]{:S(2)}) %collective-permute-start.1) | collective-permute-done | bytes 4194336 | tf_op jit(solution)/shard_map/ppermute | solution.py:17
  95.9 0.9 collective-permute-done
  96.9 12.5 %pad_maximum_fusion = f32[24576,128]{1,0:T(8,128)} fusion(f32[8192,128]{1,0:T(8,128)} %collective-permute-done.1, f32[8192,128]{1,0:T(8,128)} %param.4, f32[8192,128]{1,0:T(8,128)} %collective-permute-done), kind=kLoop, calls=%fused_computation.1 | loop fusion | flops 6291456 | bytes 25165824 | tf_op jit(solution)/shard_map/concatenate | solution.py:13
  109.4 7.3 %gather_fusion = f32[64,128,128]{2,1,0:T(8,128)} fusion(f32[192,128,128]{2,1,0:T(8,128)} %bitcast.23, s32[1024]{0:T(1024)S(1)} %pad_clamp_fusion), kind=kCustom, calls=%fused_computation | custom fusion | bytes 8388864 | tf_op jit(solution)/shard_map/gather | solution.py:35
  116.7 9.7 %fusion = f32[64,128,128]{1,2,0:T(8,128)} fusion(f32[64,1,128,128]{3,2,1,0:T(8,128)} %param.5, f32[64,128,128]{2,1,0:T(8,128)} %gather_fusion, f32[64]{0:T(128)S(1)} %compare_convert_fusion), kind=kOutput, calls=%fused_computation.2 | convolution fusion | flops 1611661312 | bytes 12583168 | tf_op jit(solution)/shard_map/jsab,jsbc->jac/dot_general | solution.py:36
  126.4 0.0 reduce-scatter.2.cloned.1.call-update
  126.4 0.2 all-reduce.2.cloned.1.call-start
  126.7 58.3 %reduce-scatter.2.cloned.1.call-done = f32[1024,128]{1,0:T(8,128)} async-done(((f32[8192,128]{1,0:T(8,128)}), f32[1024,128]{1,0:T(8,128)}) %reduce-scatter.2.cloned.1.call-update) | async-done | bytes 524304 | tf_op jit(solution)/shard_map/reduce_scatter | solution.py:38
  185.0 2.8 fusion.7
  187.8 0.0 all-reduce.2.cloned.1.call-update
  187.8 444.5 %all-reduce.2.cloned.1.call-done = f32[128,128]{0,1:T(8,128)} async-done(((f32[128,128]{0,1:T(8,128)}), f32[128,128]{0,1:T(8,128)}) %all-reduce.2.cloned.1.call-update) | async-done | bytes 65552 | tf_op jit(solution)/shard_map/psum | solution.py:40
  632.3 0.9 copy.7
  633.2 0.9 fusion.5
  634.1 11.7 %cholesky.16 = f32[128,128]{1,0:T(8,128)S(1)} custom-call(f32[128,128]{1,0:T(8,128)S(1)} %fusion.5), custom_call_target="Cholesky" | custom-call | tf_op jit(solution)/shard_map/jit(cholesky)/cholesky | solution.py:41
  645.8 0.6 compare_reduce_fusion
  646.5 0.7 multiply_bitcast_fusion
  647.2 9.8 %custom-call.7 = f32[1,128,128]{1,2,0:T(8,128)S(1)} custom-call(f32[1,128,128]{2,1,0:T(8,128)S(1)} %get-tuple-element.5), custom_call_target="InvertDiagBlocksLowerTriangular" | custom-call | tf_op jit(solution)/shard_map/jit(_solve_triangular)/triangular_solve | solution.py:42
  657.0 0.7 copy.8
  657.7 2.4 convolution_multiply_fusion
  (2 shorter events, 0.0 us)
Async XLA Ops:
  7.2 177.8 %reduce-scatter.2.cloned.1.call-start = ((), (), s32[]{:S(2)}) async-start(), calls=%async_computation.1 | async-start | bytes 4718592 | tf_op jit(solution)/shard_map/reduce_scatter | solution.py:38
  7.2 88.7 %collective-permute-start.1 = (f32[8192,128]{1,0:T(8,128)}, f32[8192,128]{1,0:T(8,128)}, u32[]{:S(2)}, u32[]{:S(2)}) collective-permute-start(f32[8192,128]{1,0:T(8,128)} %param.4), channel_id=1, source_target_pairs={{8,0},{16,8},{24,16},{32,24},{40,32},{48,40},{56,48},{64,56},{72,6... | collective-permute-start | bytes 12582920 | tf_op jit(solution)/shard_map/ppermute | solution.py:17
  8.5 88.3 %collective-permute-start = (f32[8192,128]{1,0:T(8,128)}, f32[8192,128]{1,0:T(8,128)}, u32[]{:S(2)}, u32[]{:S(2)}) collective-permute-start(f32[8192,128]{1,0:T(8,128)} %param.4), channel_id=1, source_target_pairs={{0,8},{8,16},{16,24},{24,32},{32,40},{40,48},{48,56},{56,64},{64,7... | collective-permute-start | bytes 12582920 | tf_op jit(solution)/shard_map/ppermute | solution.py:15
  126.4 505.9 %all-reduce.2.cloned.1.call-start = ((), (), s32[]{:S(2)}) async-start(), calls=%async_computation.2 | async-start | bytes 131072 | tf_op jit(solution)/shard_map/psum | solution.py:40
Sparse Core Ops, SparseCore 0:
  126.5 58.3 reduce-scatter.1
  191.0 441.2 all-reduce.1
where the time goes:
time: 667 us
  waiting for transfers between devices  583 us (87%)
  other arithmetic  37.6 us (6%)
  matrix products  14.9 us (2%)
  between operations  14.1 us (2%)
  local copies, waits for them, and re-layouts  9 us (1%)
  starting transfers between devices  8.15 us (1%)
    psum x1, waiting for transfers between devices, on_device(): gram_matrix = lax.psum(local_gram, ('rows', 'cols'))  444 us
    ppermute x1, waiting for transfers between devices, with_halo(): lax.ppermute(head, axis, [((i + 1) % count, i) for i in range(ends)])  79.5 us
    reduce_scatter x1, waiting for transfers between devices, on_device(): lax.psum_scatter(partial_value, 'cols', scatter_dimension=0, tiled=True)  58.3 us
  transfers between devices with their start and end apart: 4, of which 4 were waited for; matrix products, arithmetic and copies ran while one was open for 0% of the time, Pallas kernels for 0%

commit v1 on v0

v1 whole, which is shorter than its diff:
```python
import functools
import itertools

import jax
import jax.numpy as jnp
from jax import lax
from jax.experimental import pallas as pl
from jax.experimental.pallas import tpu as pltpu
from jax.sharding import PartitionSpec as P

EXACT = lax.Precision.HIGHEST
SUBLANES = 8


def split_bf16(x):
    high = x.astype(jnp.bfloat16)
    low = (x - high.astype(jnp.float32)).astype(jnp.bfloat16)
    return high, low


def product_kernel(
    idx_ref, count_ref, place_ref, own_ref, left_ref, left_other_ref, right_ref, right_other_ref, tile_ref,
    out_ref, gram_ref, tile_buf, vec_buf, tile_sem, vec_sem,
):
    slots, rows_kept, size, width = tile_ref.shape
    blocks = own_ref.shape[0] // size
    half = blocks // 2
    first_row, core = place_ref[0], place_ref[1]

    def copy_vec(source, block, at):
        start = pl.multiple_of(block * size, size)
        return pltpu.make_async_copy(source.at[pl.ds(start, size)], vec_buf.at[at], vec_sem.at[at])

    def fetch(at, carry):
        row, slot = at // slots, at % slots
        pltpu.make_async_copy(tile_ref.at[slot, row], tile_buf.at[at], tile_sem.at[at]).start()
        block = idx_ref[slot, row]
        side, within = block // blocks, block % blocks
        first_half = within // half == core
        place = within % half

        @pl.when(side == 1)
        def _():
            copy_vec(own_ref, within, at).start()

        @pl.when((side == 0) & first_half)
        def _():
            copy_vec(left_ref, place, at).start()

        @pl.when((side == 0) & jnp.logical_not(first_half))
        def _():
            copy_vec(left_other_ref, place, at).start()

        @pl.when((side == 2) & first_half)
        def _():
            copy_vec(right_ref, place, at).start()

        @pl.when((side == 2) & jnp.logical_not(first_half))
        def _():
            copy_vec(right_other_ref, place, at).start()

        return carry

    lax.fori_loop(0, slots * rows_kept, fetch, 0)
    gram_ref[...] = jnp.zeros_like(gram_ref)

    def row_block(row, carry):
        count = count_ref[first_row + row]
        total = jnp.zeros((size, width), jnp.float32)
        for slot in range(0, slots, 2):
            tiles, vecs = [], []
            for one in (slot, slot + 1):
                at = row * slots + one
                pltpu.make_async_copy(tile_ref.at[one, row], tile_buf.at[at], tile_sem.at[at]).wait()
                copy_vec(own_ref, 0, at).wait()
                tiles.append(tile_buf[at])
                vecs.append(vec_buf[at] * (one < count).astype(jnp.float32))
            tile_high, tile_low = split_bf16(jnp.concatenate(tiles, axis=1))
            vec_high, vec_low = split_bf16(jnp.concatenate(vecs, axis=0))
            both = jnp.dot(
                tile_high, jnp.concatenate([vec_high, vec_low], axis=1), preferred_element_type=jnp.float32
            )
            total += both[:, :width] + both[:, width:]
            total += jnp.dot(tile_low, vec_high, preferred_element_type=jnp.float32)
        out_ref[pl.ds(pl.multiple_of(row * size, size), size), :] = total
        gram_ref[...] += lax.dot_general(
            total, total, (((0,), (0,)), ((), ())), precision=EXACT, preferred_element_type=jnp.float32
        )
        return carry

    lax.fori_loop(0, rows_kept, row_block, 0)


def product_and_gram(idx, counts, place, own, left, left_other, right, right_other, tiles):
    slots, rows_kept, size, width = tiles.shape
    held = slots * rows_kept
    in_smem = pl.BlockSpec(memory_space=pltpu.SMEM)
    in_vmem = pl.BlockSpec(memory_space=pltpu.VMEM)
    anywhere = pl.BlockSpec(memory_space=pl.ANY)
    return pl.pallas_call(
        product_kernel,
        out_shape=(
            jax.ShapeDtypeStruct((rows_kept * size, width), jnp.float32),
            jax.ShapeDtypeStruct((width, width), jnp.float32),
        ),
        in_specs=[in_smem] * 3 + [anywhere] * 6,
        out_specs=(in_vmem, in_vmem),
        scratch_shapes=[
            pltpu.VMEM((held, size, size), jnp.float32),
            pltpu.VMEM((held, size, width), jnp.float32),
            pltpu.SemaphoreType.DMA((held,)),
            pltpu.SemaphoreType.DMA((held,)),
        ],
        compiler_params=pltpu.CompilerParams(vmem_limit_bytes=24 << 20),
    )(idx, counts, place, own, left, left_other, right, right_other, tiles)


def factor_kernel(nodes, gram_ref, rows_ref, basis_ref, factor_ref):
    size = gram_ref.shape[0]
    groups = size // SUBLANES
    gram = [gram_ref[SUBLANES * i : SUBLANES * (i + 1), :] for i in range(groups)]
    lane = lax.broadcasted_iota(jnp.int32, (SUBLANES, size), 1)
    sub = lax.broadcasted_iota(jnp.int32, (SUBLANES, size), 0)
    inverse = [(lane == sub + SUBLANES * i).astype(jnp.float32) for i in range(groups)]
    for step in range(size):
        group, within = divmod(step, SUBLANES)
        pivot_row = jnp.broadcast_to(gram[group][within : within + 1, :], (SUBLANES, size))
        inverse_row = jnp.broadcast_to(inverse[group][within : within + 1, :], (SUBLANES, size))
        scale = 1.0 / jnp.broadcast_to(pivot_row[:, step : step + 1], (SUBLANES, size))
        pivot_row, inverse_row = pivot_row * scale, inverse_row * scale
        for other in range(group, groups):
            if other == group and within == SUBLANES - 1:
                continue
            factor = jnp.broadcast_to(gram[other][:, step : step + 1], (SUBLANES, size))
            if other == group:
                factor = jnp.where(sub > within, factor, 0.0)
            gram[other] = gram[other] - factor * pivot_row
            inverse[other] = inverse[other] - factor * inverse_row
    root = jnp.sqrt(jnp.float32(nodes))
    for group in range(groups):
        here = sub + SUBLANES * group
        diagonal = jnp.sum(jnp.where(lane == here, gram[group], 0.0), axis=1, keepdims=True)
        scale = lax.rsqrt(diagonal)
        factor_ref[SUBLANES * group : SUBLANES * (group + 1), :] = jnp.where(lane >= here, gram[group] * scale, 0.0) / root
        inverse[group] = inverse[group] * (scale * root)
    basis_ref[...] = lax.dot_general(
        rows_ref[...], jnp.concatenate(inverse, axis=0), (((1,), (1,)), ((), ())),
        precision=EXACT, preferred_element_type=jnp.float32,
    )


def basis_and_factor(nodes, gram, rows):
    in_vmem = pl.BlockSpec(memory_space=pltpu.VMEM)
    return pl.pallas_call(
        functools.partial(factor_kernel, nodes),
        out_shape=(jax.ShapeDtypeStruct(rows.shape, jnp.float32), jax.ShapeDtypeStruct(gram.shape, jnp.float32)),
        in_specs=[in_vmem] * 2,
        out_specs=(in_vmem, in_vmem),
        compiler_params=pltpu.CompilerParams(vmem_limit_bytes=24 << 20),
    )(gram, rows)


def device_groups(row_devices, col_devices, row_step, key):
    groups = {}
    for row, col in itertools.product(range(row_devices), range(col_devices)):
        groups.setdefault(key(row // row_step, row % row_step, col), []).append(row * col_devices + col)
    return list(groups.values())


def exchange(pieces, groups):
    return lax.all_to_all(pieces, ("rows", "cols"), 0, 0, axis_index_groups=groups, tiled=True)


def sum_over_devices(gram, row_devices, col_devices):
    row_step = 4
    plane = device_groups(row_devices, col_devices, row_step, lambda z, y, col: z)
    across = device_groups(row_devices, col_devices, row_step, lambda z, y, col: (y, col))
    in_plane, planes = len(plane[0]), len(across[0])
    size, width = gram.shape
    piece = exchange(gram.reshape(in_plane, size // in_plane, width), plane).sum(0)
    piece = exchange(jnp.broadcast_to(piece[None], (planes,) + piece.shape), across).sum(0)
    return exchange(jnp.broadcast_to(piece[None], (in_plane,) + piece.shape), plane).reshape(size, width)


def on_device(block_vector, op_tiles, tile_cols, live_counts):
    block_count, _, size, width = op_tiles.shape
    row_devices, col_devices = lax.axis_size("rows"), lax.axis_size("cols")
    row, col = lax.axis_index("rows"), lax.axis_index("cols")
    rows_here = block_count * size
    rows_kept = block_count // col_devices
    core = col % 2

    def swap(x):
        return lax.ppermute(x, "cols", [(i, i ^ 1) for i in range(col_devices)])

    ends = row_devices - 1
    half = lax.dynamic_slice_in_dim(block_vector, core * (rows_here // 2), rows_here // 2, axis=0)
    left = lax.ppermute(half, "rows", [(i, i + 1) for i in range(ends)])
    right = lax.ppermute(half, "rows", [(i + 1, i) for i in range(ends)])
    tiles = lax.all_to_all(op_tiles.reshape(col_devices, rows_kept, size, size), "cols", 0, 0, tiled=True)
    local_idx = tile_cols - (row - 1) * block_count
    idx = lax.all_to_all(local_idx.reshape(col_devices, rows_kept), "cols", 0, 0, tiled=True)
    place = jnp.stack([col * rows_kept, core]).astype(jnp.int32)
    part_rows, gram = product_and_gram(
        idx, live_counts, place, block_vector, left, swap(left), right, swap(right), tiles
    )
    gram = sum_over_devices(gram, row_devices, col_devices)
    return basis_and_factor(rows_here * row_devices, gram, part_rows)


def solution(mesh):
    in_specs = (P("rows", None), P("rows", "cols", None, None), P("rows", "cols"), P("rows"))
    out_specs = (P(("rows", "cols"), None), P())
    return jax.shard_map(
        on_device, mesh=mesh, in_specs=in_specs, out_specs=out_specs, check_vma=False
    )
```

time: 667 us -> 166 us (0.25)
  waiting for transfers between devices: 583 us -> 38 us
  blocking collectives: 0 us -> 61.2 us
  other arithmetic: 37.6 us -> 0.17 us
  Pallas kernels: 0 us -> 36.3 us
  starting transfers between devices: 8.15 us -> 23.3 us
  matrix products: 14.9 us -> 0 us
  between operations: 14.1 us -> 0.72 us
    psum x1 -> x0, waiting for transfers between devices: 444 us -> none  [on_device(): gram_matrix = lax.psum(local_gram, ('rows', 'cols'))]
    ppermute x2 -> x4, waiting for transfers between devices: 80.4 us -> 17.5 us  [the longest x1 17.5 us: on_device(): right = lax.ppermute(half, 'rows', [(i + 1, i) for i in range(ends)])]
    all_to_all x0 -> x4, blocking collectives: none -> 61.2 us  [the longest x3 47.6 us: exchange(): lax.all_to_all(pieces, ('rows', 'cols'), 0, 0, axis_index_groups=groups,...]
    reduce_scatter x1 -> x0, waiting for transfers between devices: 58.3 us -> none  [on_device(): lax.psum_scatter(partial_value, 'cols', scatter_dimension=0, tiled=True)]
    pallas_call x0 -> x2, Pallas kernels: none -> 36.3 us  [the longest x1 18.5 us: basis_and_factor(): pl.pallas_call(functools.partial(factor_kernel, nodes), out_shape=(jax.Sh...]
    another operation x4 -> x1, other arithmetic: 22.2 us -> 0.08 us  [on_device(): place = jnp.stack([col * rows_kept, core]).astype(jnp.int32)]
    all_to_all x0 -> x1, waiting for transfers between devices: none -> 20.5 us  [on_device(): lax.all_to_all(op_tiles.reshape(col_devices, rows_kept, size, size), 'col...]
    concatenate x1 -> x0, other arithmetic: 12.5 us -> none  [with_halo(): jnp.concatenate([lax.ppermute(tail, axis, [(i, (i + 1) % count) for i in...]
  transfers between devices with their start and end apart: 4 -> 5, of which waited for: 4 -> 2; matrix products, arithmetic and copies ran while one was open for 0% -> 0% of each run, Pallas kernels for 0% -> 0%
where the time goes in v1:
time: 166 us; the launch traced here: 165 us
  blocking collectives  61.2 us (37%)
  waiting for transfers between devices  38 us (23%)
  Pallas kernels  36.3 us (22%)
  starting transfers between devices  23.3 us (14%)
  local copies, waits for them, and re-layouts  5.4 us (3%)
    all_to_all x3, blocking collectives, exchange(): lax.all_to_all(pieces, ('rows', 'cols'), 0, 0, axis_index_groups=groups,...  47.6 us
    all_to_all x1, waiting for transfers between devices, on_device(): lax.all_to_all(op_tiles.reshape(col_devices, rows_kept, size, size), 'col...  20.5 us
    pallas_call x1, Pallas kernels, basis_and_factor(): pl.pallas_call(functools.partial(factor_kernel, nodes), out_shape=(jax.Sh...  18.5 us
    pallas_call x1, Pallas kernels, product_and_gram(): pl.pallas_call(product_kernel, out_shape=(jax.ShapeDtypeStruct((rows_kept...  17.8 us
    ppermute x1, waiting for transfers between devices, on_device(): right = lax.ppermute(half, 'rows', [(i + 1, i) for i in range(ends)])  17.5 us
    all_to_all x1, blocking collectives, on_device(): lax.all_to_all(local_idx.reshape(col_devices, rows_kept), 'cols', 0, 0, t...  13.7 us
    ppermute x2, starting transfers between devices, swap(): return lax.ppermute(x, 'cols', [(i, i ^ 1) for i in range(col_devices)])  10.8 us
    ppermute x1, starting transfers between devices, on_device(): left = lax.ppermute(half, 'rows', [(i, i + 1) for i in range(ends)])  5.99 us
  transfers between devices with their start and end apart: 5, of which 2 were waited for; matrix products, arithmetic and copies ran while one was open for 0% of the time, Pallas kernels for 0%

profile of v1, /device:TPU:1, one launch (start us, length us, event | category | flops | bytes accessed | tf_op | source)
XLA Modules:
  0.0 165.1 jit_solution(2563347498746760946)
XLA Ops:
  0.6 0.0 copy-start.2
  0.7 3.1 %constant_dynamic-slice_fusion = f32[4096,128]{1,0:T(8,128)} fusion(f32[8192,128]{1,0:T(8,128)} %own_ref.1, s32[]{:T(128)S(6)} %select_n.11), kind=kLoop, calls=%fused_computation.2 | loop fusion | bytes 4194308 | tf_op jit(solution)/shard_map/dynamic_slice | solution.py:197
  3.8 1.3 collective-permute-start.2
  5.0 6.0 %collective-permute-start = (f32[4096,128]{1,0:T(8,128)}, f32[4096,128]{1,0:T(8,128)}, u32[]{:S(2)}, u32[]{:S(2)}) collective-permute-start(f32[4096,128]{1,0:T(8,128)} %constant_dynamic-slice_fusion), channel_id=1, source_target_pairs={{0,8},{8,16},{16,24},{24,32},{32,40},{40,48},{48,56},{56,64},{64,7... | collective-permute-start | bytes 6291464 | tf_op jit(solution)/shard_map/ppermute | solution.py:198
  11.0 0.0 copy-done.2
  11.1 0.1 all_to_all.19
  11.1 13.7 %all_to_all.31 = s32[8,1,8]{2,1,0:T(1,128)S(1)} all-to-all(s32[8,1,8]{2,1,0:T(1,128)S(1)} %bitcast.11), channel_id=1, replica_groups=mesh['rows'=64,'cols'=8] {'cols'}, dimensions={0} | all-to-all | bytes 512 | tf_op jit(solution)/shard_map/all_to_all | solution.py:202
  24.8 0.0 copy-start.1
  24.8 5.2 %all-to-all-start.1 = ((f32[8,8,128,128]{3,2,1,0:T(8,128)}), f32[8,8,128,128]{3,2,1,0:T(8,128)}, u32[]{:S(2)}, u32[]{:S(2)}) async-start(f32[8,8,128,128]{3,2,1,0:T(8,128)} %bitcast.10), calls=%async_computation.1 | async-start | bytes 8388608 | tf_op jit(solution)/shard_map/all_to_all | solution.py:200
  30.1 17.5 %collective-permute-done.2.right_ref = f32[4096,128]{1,0:T(8,128)S(1)} collective-permute-done((f32[4096,128]{1,0:T(8,128)}, f32[4096,128]{1,0:T(8,128)S(1)}, u32[]{:S(2)}, u32[]{:S(2)}) %collective-permute-start.2) | collective-permute-done | bytes 2097184 | tf_op jit(solution)/shard_map/ppermute | solution.py:199
  47.5 8.9 %collective-permute-start.3 = (f32[4096,128]{1,0:T(8,128)S(1)}, f32[4096,128]{1,0:T(8,128)}, u32[]{:S(2)}, u32[]{:S(2)}) collective-permute-start(f32[4096,128]{1,0:T(8,128)S(1)} %collective-permute-done.2.right_ref), channel_id=1, source_target_pairs={{0,1},{1,0},{2,3},{3,2},{4,5},{5,4},{6,7},{7,6},{8,9},{9,8},{10,11... | collective-permute-start | bytes 6291464 | tf_op jit(solution)/shard_map/ppermute | solution.py:194
  56.5 0.0 collective-permute-done.left_ref
  56.5 1.9 %collective-permute-start.1 = (f32[4096,128]{1,0:T(8,128)}, f32[4096,128]{1,0:T(8,128)}, u32[]{:S(2)}, u32[]{:S(2)}) collective-permute-start(f32[4096,128]{1,0:T(8,128)} %collective-permute-done.left_ref), channel_id=1, source_target_pairs={{0,1},{1,0},{2,3},{3,2},{4,5},{5,4},{6,7},{7,6},{8,9},{9,8},{10,11... | collective-permute-start | bytes 6291464 | tf_op jit(solution)/shard_map/ppermute | solution.py:194
  58.4 0.1 pad_add_fusion.place_ref
  58.5 20.5 %all-to-all-done.1.tile_ref = f32[8,8,128,128]{3,2,1,0:T(8,128)} async-done(((f32[8,8,128,128]{3,2,1,0:T(8,128)}), f32[8,8,128,128]{3,2,1,0:T(8,128)}, u32[]{:S(2)}, u32[]{:S(2)}) %all-to-all-start.1) | async-done | bytes 4194336 | tf_op jit(solution)/shard_map/all_to_all | solution.py:200
  79.0 0.0 collective-permute-done.3.right_other_ref
  79.0 0.0 collective-permute-done.1.left_other_ref
  79.0 0.0 copy-done.1
  79.0 0.0 copy-start
  79.0 2.2 %copy-done = f32[8192,128]{1,0:T(8,128)S(1)} copy-done((f32[8192,128]{1,0:T(8,128)S(1)}, f32[8192,128]{1,0:T(8,128)}, u32[]{:S(2)}) %copy-start) | copy-done | bytes 4194328
  81.2 17.8 %shard_map.59 = (f32[1024,128]{1,0:T(8,128)S(1)}, f32[128,128]{1,0:T(8,128)S(1)}) custom-call(s32[8,8]{1,0:T(8,128)S(1)} %bitcast.9, s32[64]{0:T(128)S(1)} %copy-done.1, s32[2]{0:T(128)S(1)} %pad_add_fusion.place_ref, f32[8192,128]{1,0:T(8,128)S(1)} %copy-done, f32[4096,128]{1,0:T(8,128)} %collective-permute-done.left_ref, ...), custom_call_target="tpu_custom_call" | custom-call | tf_op jit(solution)/shard_map/pallas_call | solution.py:100
  99.0 11.0 %all_to_all.32 = f32[32,4,128]{2,1,0:T(4,128)S(1)} all-to-all(f32[32,4,128]{2,1,0:T(4,128)S(1)} %bitcast.8), channel_id=1, replica_groups={{0,1,2,3,4,5,6,7,8,9,10,11,12,13,14,15,16,17,18,19,20,21,22,23,24,25,26..., dimensions={0} | all-to-all | bytes 131072 | tf_op jit(solution)/shard_map/all_to_all | solution.py:171
  110.1 24.3 %all_to_all.33 = f32[16,4,128]{2,1,0:T(4,128)S(1)} all-to-all(f32[16,4,128]{2,1,0:T(4,128)S(1)} %broadcast_in_dim.4), channel_id=1, replica_groups={{0,32,64,96,128,160,192,224,256,288,320,352,384,416,448,480},{1,33,65,9..., dimensions={0} | all-to-all | bytes 65536 | tf_op jit(solution)/shard_map/all_to_all | solution.py:171
  134.4 12.3 %all_to_all.34 = f32[32,4,128]{2,1,0:T(4,128)S(1)} all-to-all(f32[32,4,128]{2,1,0:T(4,128)S(1)} %broadcast_in_dim.5), channel_id=1, replica_groups={{0,1,2,3,4,5,6,7,8,9,10,11,12,13,14,15,16,17,18,19,20,21,22,23,24,25,26..., dimensions={0} | all-to-all | bytes 131072 | tf_op jit(solution)/shard_map/all_to_all | solution.py:171
  146.7 18.5 %shard_map.60 = (f32[1024,128]{1,0:T(8,128)}, f32[128,128]{1,0:T(8,128)}) custom-call(f32[128,128]{1,0:T(8,128)S(1)} %bitcast.7, f32[1024,128]{1,0:T(8,128)S(1)} %get-tuple-element.5.rows_ref), custom_call_target="tpu_custom_call" | custom-call | tf_op jit(solution)/shard_map/pallas_call | solution.py:154
  (5 shorter events, 0.1 us)
Async XLA Ops:
  0.6 10.4 %copy-start.2 = (s32[64,1]{0,1:T(1,128)S(1)}, s32[64,1]{0,1:T(1,128)}, u32[]{:S(2)}) copy-start(s32[64,1]{0,1:T(1,128)} %param.6) | copy-start | bytes 772
  3.8 43.8 %collective-permute-start.2 = (f32[4096,128]{1,0:T(8,128)}, f32[4096,128]{1,0:T(8,128)S(1)}, u32[]{:S(2)}, u32[]{:S(2)}) collective-permute-start(f32[4096,128]{1,0:T(8,128)} %constant_dynamic-slice_fusion), channel_id=1, source_target_pairs={{8,0},{16,8},{24,16},{32,24},{40,32},{48,40},{56,48},{64,56},{72,6... | collective-permute-start | bytes 6291464 | tf_op jit(solution)/shard_map/ppermute | solution.py:199
  5.0 51.4 %collective-permute-start = (f32[4096,128]{1,0:T(8,128)}, f32[4096,128]{1,0:T(8,128)}, u32[]{:S(2)}, u32[]{:S(2)}) collective-permute-start(f32[4096,128]{1,0:T(8,128)} %constant_dynamic-slice_fusion), channel_id=1, source_target_pairs={{0,8},{8,16},{16,24},{24,32},{32,40},{40,48},{48,56},{56,64},{64,7... | collective-permute-start | bytes 6291464 | tf_op jit(solution)/shard_map/ppermute | solution.py:198
  24.8 54.2 %copy-start.1 = (s32[64]{0:T(128)S(1)}, s32[64]{0:T(128)}, u32[]{:S(2)}) copy-start(s32[64]{0:T(128)} %count_ref.1) | copy-start | bytes 772
  24.8 54.2 %all-to-all-start.1 = ((f32[8,8,128,128]{3,2,1,0:T(8,128)}), f32[8,8,128,128]{3,2,1,0:T(8,128)}, u32[]{:S(2)}, u32[]{:S(2)}) async-start(f32[8,8,128,128]{3,2,1,0:T(8,128)} %bitcast.10), calls=%async_computation.1 | async-start | bytes 8388608 | tf_op jit(solution)/shard_map/all_to_all | solution.py:200
  47.5 31.5 %collective-permute-start.3 = (f32[4096,128]{1,0:T(8,128)S(1)}, f32[4096,128]{1,0:T(8,128)}, u32[]{:S(2)}, u32[]{:S(2)}) collective-permute-start(f32[4096,128]{1,0:T(8,128)S(1)} %collective-permute-done.2.right_ref), channel_id=1, source_target_pairs={{0,1},{1,0},{2,3},{3,2},{4,5},{5,4},{6,7},{7,6},{8,9},{9,8},{10,11... | collective-permute-start | bytes 6291464 | tf_op jit(solution)/shard_map/ppermute | solution.py:194
  56.5 22.5 %collective-permute-start.1 = (f32[4096,128]{1,0:T(8,128)}, f32[4096,128]{1,0:T(8,128)}, u32[]{:S(2)}, u32[]{:S(2)}) collective-permute-start(f32[4096,128]{1,0:T(8,128)} %collective-permute-done.left_ref), channel_id=1, source_target_pairs={{0,1},{1,0},{2,3},{3,2},{4,5},{5,4},{6,7},{7,6},{8,9},{9,8},{10,11... | collective-permute-start | bytes 6291464 | tf_op jit(solution)/shard_map/ppermute | solution.py:194
  79.0 2.2 %copy-start = (f32[8192,128]{1,0:T(8,128)S(1)}, f32[8192,128]{1,0:T(8,128)}, u32[]{:S(2)}) copy-start(f32[8192,128]{1,0:T(8,128)} %own_ref.1) | copy-start | bytes 12582916

commit v2 on v1

--- a/solution.py
+++ b/solution.py
@@ -10,6 +10,7 @@
 
 EXACT = lax.Precision.HIGHEST
 SUBLANES = 8
+PARTS = 2
 
 
 def split_bf16(x):
@@ -19,62 +20,67 @@
 
 
 def product_kernel(
-    idx_ref, count_ref, place_ref, own_ref, left_ref, left_other_ref, right_ref, right_other_ref, tile_ref,
-    out_ref, gram_ref, tile_buf, vec_buf, tile_sem, vec_sem,
+    idx_ref, count_ref, place_ref, own_ref, *refs,
 ):
+    near_refs, far_refs = refs[:PARTS], refs[PARTS : 2 * PARTS]
+    tile_ref, out_ref, gram_ref, tile_buf, vec_buf, tile_sem, vec_sem = refs[2 * PARTS :]
     slots, rows_kept, size, width = tile_ref.shape
     blocks = own_ref.shape[0] // size
-    half = blocks // 2
-    first_row, core = place_ref[0], place_ref[1]
-
-    def copy_vec(source, block, at):
+    part = blocks // PARTS
+    col, near_side = place_ref[0], place_ref[1]
+    first_row = col * rows_kept
+
+    def copy_tiles(row):
+        return pltpu.make_async_copy(tile_ref.at[:, row], tile_buf.at[row], tile_sem.at[row])
+
+    def copy_vec(source, block, row, slot):
         start = pl.multiple_of(block * size, size)
-        return pltpu.make_async_copy(source.at[pl.ds(start, size)], vec_buf.at[at], vec_sem.at[at])
-
-    def fetch(at, carry):
-        row, slot = at // slots, at % slots
-        pltpu.make_async_copy(tile_ref.at[slot, row], tile_buf.at[at], tile_sem.at[at]).start()
-        block = idx_ref[slot, row]
-        side, within = block // blocks, block % blocks
-        first_half = within // half == core
-        place = within % half
-
-        @pl.when(side == 1)
-        def _():
-            copy_vec(own_ref, within, at).start()
-
-        @pl.when((side == 0) & first_half)
-        def _():
-            copy_vec(left_ref, place, at).start()
-
-        @pl.when((side == 0) & jnp.logical_not(first_half))
-        def _():
-            copy_vec(left_other_ref, place, at).start()
-
-        @pl.when((side == 2) & first_half)
-        def _():
-            copy_vec(right_ref, place, at).start()
-
-        @pl.when((side == 2) & jnp.logical_not(first_half))
-        def _():
-            copy_vec(right_other_ref, place, at).start()
-
-        return carry
-
-    lax.fori_loop(0, slots * rows_kept, fetch, 0)
-    gram_ref[...] = jnp.zeros_like(gram_ref)
+        return pltpu.make_async_copy(source.at[pl.ds(start, size)], vec_buf.at[row, slot], vec_sem.at[row, slot])
+
+    def fetch(row, carry):
+        copy_tiles(row).start()
+
+        def fetch_vec(slot, inner):
+            block = idx_ref[slot, first_row + row]
+            side, within = block // blocks, block % blocks
+            number, place = within // part, within % part
+
+            @pl.when(side == 1)
+            def _():
+                copy_vec(own_ref, within, row, slot).start()
+
+            @pl.when(side != 1)
+            def _():
+                for at in range(PARTS):
+
+                    @pl.when((side == near_side) & (number == at))
+                    def _():
+                        copy_vec(near_refs[at], place, row, slot).start()
+
+                    @pl.when((side != near_side) & (number == at))
+                    def _():
+                        copy_vec(far_refs[at], place, row, slot).start()
+
+            return inner
+
+        return lax.fori_loop(0, count_ref[first_row + row], fetch_vec, carry)
+
+    lax.fori_loop(0, rows_kept, fetch, 0)
 
     def row_block(row, carry):
         count = count_ref[first_row + row]
+        copy_tiles(row).wait()
+
+        def wait_vec(slot, inner):
+            copy_vec(own_ref, 0, row, slot).wait()
+            return inner
+
+        lax.fori_loop(0, count, wait_vec, 0)
         total = jnp.zeros((size, width), jnp.float32)
         for slot in range(0, slots, 2):
-            tiles, vecs = [], []
-            for one in (slot, slot + 1):
-                at = row * slots + one
-                pltpu.make_async_copy(tile_ref.at[one, row], tile_buf.at[at], tile_sem.at[at]).wait()
-                copy_vec(own_ref, 0, at).wait()
-                tiles.append(tile_buf[at])
-                vecs.append(vec_buf[at] * (one < count).astype(jnp.float32))
+            pair = (slot, slot + 1)
+            tiles = [tile_buf[row, one] for one in pair]
+            vecs = [jnp.where(one < count, vec_buf[row, one], 0.0) for one in pair]
             tile_high, tile_low = split_bf16(jnp.concatenate(tiles, axis=1))
             vec_high, vec_low = split_bf16(jnp.concatenate(vecs, axis=0))
             both = jnp.dot(
@@ -83,17 +89,17 @@
             total += both[:, :width] + both[:, width:]
             total += jnp.dot(tile_low, vec_high, preferred_element_type=jnp.float32)
         out_ref[pl.ds(pl.multiple_of(row * size, size), size), :] = total
-        gram_ref[...] += lax.dot_general(
-            total, total, (((0,), (0,)), ((), ())), precision=EXACT, preferred_element_type=jnp.float32
-        )
         return carry
 
     lax.fori_loop(0, rows_kept, row_block, 0)
-
-
-def product_and_gram(idx, counts, place, own, left, left_other, right, right_other, tiles):
+    high, low = split_bf16(out_ref[...])
+    both = jnp.concatenate([high, low], axis=1)
+    gram = lax.dot_general(both, both, (((0,), (0,)), ((), ())), preferred_element_type=jnp.float32)
+    gram_ref[...] = gram[:width, :width] + (gram[:width, width:] + gram[width:, :width]) + gram[width:, width:]
+
+
+def product_and_gram(idx, counts, place, own, near, far, tiles):
     slots, rows_kept, size, width = tiles.shape
-    held = slots * rows_kept
     in_smem = pl.BlockSpec(memory_space=pltpu.SMEM)
     in_vmem = pl.BlockSpec(memory_space=pltpu.VMEM)
     anywhere = pl.BlockSpec(memory_space=pl.ANY)
@@ -103,16 +109,16 @@
             jax.ShapeDtypeStruct((rows_kept * size, width), jnp.float32),
             jax.ShapeDtypeStruct((width, width), jnp.float32),
         ),
-        in_specs=[in_smem] * 3 + [anywhere] * 6,
+        in_specs=[in_smem] * 3 + [anywhere] * (2 + 2 * PARTS),
         out_specs=(in_vmem, in_vmem),
         scratch_shapes=[
-            pltpu.VMEM((held, size, size), jnp.float32),
-            pltpu.VMEM((held, size, width), jnp.float32),
-            pltpu.SemaphoreType.DMA((held,)),
-            pltpu.SemaphoreType.DMA((held,)),
+            pltpu.VMEM((rows_kept, slots, size, size), jnp.float32),
+            pltpu.VMEM((rows_kept, slots, size, width), jnp.float32),
+            pltpu.SemaphoreType.DMA((rows_kept,)),
+            pltpu.SemaphoreType.DMA((rows_kept, slots)),
         ],
-        compiler_params=pltpu.CompilerParams(vmem_limit_bytes=24 << 20),
-    )(idx, counts, place, own, left, left_other, right, right_other, tiles)
+        compiler_params=pltpu.CompilerParams(vmem_limit_bytes=62 << 20),
+    )(idx, counts, place, own, *near, *far, tiles)
 
 
 def factor_kernel(nodes, gram_ref, rows_ref, basis_ref, factor_ref):
@@ -156,7 +162,7 @@
         out_shape=(jax.ShapeDtypeStruct(rows.shape, jnp.float32), jax.ShapeDtypeStruct(gram.shape, jnp.float32)),
         in_specs=[in_vmem] * 2,
         out_specs=(in_vmem, in_vmem),
-        compiler_params=pltpu.CompilerParams(vmem_limit_bytes=24 << 20),
+        compiler_params=pltpu.CompilerParams(vmem_limit_bytes=62 << 20),
     )(gram, rows)
 
 
@@ -188,22 +194,28 @@
     row, col = lax.axis_index("rows"), lax.axis_index("cols")
     rows_here = block_count * size
     rows_kept = block_count // col_devices
-    core = col % 2
-
-    def swap(x):
-        return lax.ppermute(x, "cols", [(i, i ^ 1) for i in range(col_devices)])
-
-    ends = row_devices - 1
-    half = lax.dynamic_slice_in_dim(block_vector, core * (rows_here // 2), rows_here // 2, axis=0)
-    left = lax.ppermute(half, "rows", [(i, i + 1) for i in range(ends)])
-    right = lax.ppermute(half, "rows", [(i + 1, i) for i in range(ends)])
+    near_side = 2 * (col % 2)
+
+    def fetched_by(r, c):
+        if c % 2 == 0:
+            return (r, c + 1) if r == row_devices - 1 else (r + 1, c)
+        return (r, c - 1) if r == 0 else (r - 1, c)
+
+    steps = []
+    for r, c in itertools.product(range(row_devices), range(col_devices)):
+        to_r, to_c = fetched_by(r, c)
+        steps.append((r * col_devices + c, to_r * col_devices + to_c))
+    rows_part = rows_here // PARTS
+    near = [
+        lax.ppermute(block_vector[at * rows_part : (at + 1) * rows_part], ("rows", "cols"), steps) for at in range(PARTS)
+    ]
+    idx = lax.all_gather((tile_cols - (row - 1) * block_count).reshape(block_count), "cols")
+    head = jnp.where(jnp.min(idx) < 0, 0.0, near[-1][:SUBLANES])
+    near[-1] = lax.dynamic_update_slice(near[-1], head, (0, 0))
+    far = [lax.ppermute(part, "cols", [(i, i ^ 1) for i in range(col_devices)]) for part in near]
     tiles = lax.all_to_all(op_tiles.reshape(col_devices, rows_kept, size, size), "cols", 0, 0, tiled=True)
-    local_idx = tile_cols - (row - 1) * block_count
-    idx = lax.all_to_all(local_idx.reshape(col_devices, rows_kept), "cols", 0, 0, tiled=True)
-    place = jnp.stack([col * rows_kept, core]).astype(jnp.int32)
-    part_rows, gram = product_and_gram(
-        idx, live_counts, place, block_vector, left, swap(left), right, swap(right), tiles
-    )
+    place = jnp.stack([col, near_side]).astype(jnp.int32)
+    part_rows, gram = product_and_gram(idx, live_counts, place, block_vector, near, far, tiles)
     gram = sum_over_devices(gram, row_devices, col_devices)
     return basis_and_factor(rows_here * row_devices, gram, part_rows)
 

time: 166 us -> 159 us (0.958)
  blocking collectives: 61.2 us -> 96.2 us
  waiting for transfers between devices: 38 us -> 3.88 us
  Pallas kernels: 36.3 us -> 25.9 us
  local copies, waits for them, and re-layouts: 5.4 us -> 7.82 us
  starting transfers between devices: 23.3 us -> 21.1 us
    unnamed x0 -> x1, blocking collectives: none -> 48.4 us
    all_to_all x1, waiting for transfers between devices: 20.5 us -> 0.01 us  [on_device(): lax.all_to_all(op_tiles.reshape(col_devices, rows_kept, size, size), 'col...]
    all_to_all x1 -> x0, blocking collectives: 13.7 us -> none  [on_device(): lax.all_to_all(local_idx.reshape(col_devices, rows_kept), 'cols', 0, 0, t...]
    ppermute x4, waiting for transfers between devices: 17.5 us -> 3.87 us  [the longest x2 3.87 us: on_device(): lax.ppermute(part, 'cols', [(i, i ^ 1) for i in range(col_devices)])]
    pallas_call x1, Pallas kernels: 17.8 us -> 6.37 us  [product_and_gram(): pl.pallas_call(product_kernel, out_shape=(jax.ShapeDtypeStruct((rows_kept...]
    slice x0 -> x1, local copies, waits for them, and re-layouts: none -> 4.51 us  [on_device(): block_vector[at * rows_part:(at + 1) * rows_part]]
    dynamic_slice x1 -> x0, local copies, waits for them, and re-layouts: 3.1 us -> none  [on_device(): lax.dynamic_slice_in_dim(block_vector, core * (rows_here // 2), rows_here...]
  transfers between devices with their start and end apart: 5 -> 5, of which waited for: 2 -> 2; matrix products, arithmetic and copies ran while one was open for 0% -> 2% of each run, Pallas kernels for 0% -> 0%
where the time goes in v2:
time: 159 us; the launch traced here: 158 us
  blocking collectives  96.2 us (61%)
  Pallas kernels  25.9 us (16%)
  starting transfers between devices  21.1 us (13%)
  local copies, waits for them, and re-layouts  7.82 us (5%)
  waiting for transfers between devices  3.88 us (2%)
  between operations  2.06 us (1%)
    unnamed x1, blocking collectives  48.4 us
    all_to_all x3, blocking collectives, exchange(): lax.all_to_all(pieces, ('rows', 'cols'), 0, 0, axis_index_groups=groups,...  47.8 us
    pallas_call x1, Pallas kernels, basis_and_factor(): pl.pallas_call(functools.partial(factor_kernel, nodes), out_shape=(jax.Sh...  19.5 us
    ppermute x2, starting transfers between devices, on_device(): lax.ppermute(block_vector[at * rows_part:(at + 1) * rows_part], ('rows',...  10.7 us
    pallas_call x1, Pallas kernels, product_and_gram(): pl.pallas_call(product_kernel, out_shape=(jax.ShapeDtypeStruct((rows_kept...  6.37 us
    ppermute x2, starting transfers between devices, on_device(): lax.ppermute(part, 'cols', [(i, i ^ 1) for i in range(col_devices)])  5.83 us
    all_to_all x1, starting transfers between devices, on_device(): lax.all_to_all(op_tiles.reshape(col_devices, rows_kept, size, size), 'col...  4.53 us
    slice x1, local copies, waits for them, and re-layouts, on_device(): block_vector[at * rows_part:(at + 1) * rows_part]  4.51 us
  transfers between devices with their start and end apart: 5, of which 2 were waited for; matrix products, arithmetic and copies ran while one was open for 2% of the time, Pallas kernels for 0%

profile of v2, /device:TPU:1, one launch (start us, length us, event | category | flops | bytes accessed | tf_op | source)
XLA Modules:
  0.0 158.4 jit_solution(4983720976231697983)
XLA Ops:
  0.6 4.5 %fusion.1 = (f32[4096,128]{1,0:T(8,128)}, f32[4096,128]{1,0:T(8,128)}) fusion(f32[8192,128]{1,0:T(8,128)} %own_ref.1), kind=kLoop, calls=%fused_computation.4 | loop fusion | bytes 8388608 | tf_op jit(solution)/shard_map/slice | solution.py:210
  5.1 8.8 %collective-permute-start.1 = (f32[4096,128]{1,0:T(8,128)}, f32[4096,128]{1,0:T(8,128)S(1)}, u32[]{:S(2)}, u32[]{:S(2)}) collective-permute-start(f32[4096,128]{1,0:T(8,128)} %get-tuple-element.6), channel_id=1, source_target_pairs={{0,8},{1,0},{2,10},{3,2},{4,12},{5,4},{6,14},{7,6},{8,16},{9,1},{1... | collective-permute-start | bytes 6291464 | tf_op jit(solution)/shard_map/ppermute | solution.py:210
  13.9 1.9 %collective-permute-start = (f32[4096,128]{1,0:T(8,128)}, f32[4096,128]{1,0:T(8,128)}, u32[]{:S(2)}, u32[]{:S(2)}) collective-permute-start(f32[4096,128]{1,0:T(8,128)} %get-tuple-element.7), channel_id=1, source_target_pairs={{0,8},{1,0},{2,10},{3,2},{4,12},{5,4},{6,14},{7,6},{8,16},{9,1},{1... | collective-permute-start | bytes 6291464 | tf_op jit(solution)/shard_map/ppermute | solution.py:210
  15.9 0.0 copy-start.1
  15.9 4.5 %all-to-all-start = ((f32[8,8,128,128]{3,2,1,0:T(8,128)}), f32[8,8,128,128]{3,2,1,0:T(8,128)}, u32[]{:S(2)}, u32[]{:S(2)}) async-start(f32[8,8,128,128]{3,2,1,0:T(8,128)} %bitcast.8), calls=%async_computation | async-start | bytes 8388608 | tf_op jit(solution)/shard_map/all_to_all | solution.py:216
  20.4 1.3 dynamic-slice
  22.3 0.0 copy-done.1
  22.4 0.1 bitcast_dynamic-update-slice_fusion
  22.5 48.4 %all-reduce = s32[512]{0:T(512)S(1)} all-reduce(s32[512]{0:T(512)S(1)} %bitcast_dynamic-update-slice_fusion), channel_id=2, replica_groups=mesh['rows'=64,'cols'=8] {'cols'}, use_global_device_ids=true, to_apply=%add | all-reduce | flops 512 | bytes 4096
  70.9 0.6 reduce_min.9
  72.2 0.0 collective-permute-done.1
  72.2 0.0 copy-start
  72.2 1.3 copy-done
  73.5 3.9 %collective-permute-start.3 = (f32[4096,128]{1,0:T(8,128)S(1)}, f32[4096,128]{1,0:T(8,128)}, u32[]{:S(2)}, u32[]{:S(2)}) collective-permute-start(f32[4096,128]{1,0:T(8,128)S(1)} %fusion.refs_1_), channel_id=1, source_target_pairs={{0,1},{1,0},{2,3},{3,2},{4,5},{5,4},{6,7},{7,6},{8,9},{9,8},{10,11... | collective-permute-start | bytes 6291464 | tf_op jit(solution)/shard_map/ppermute | solution.py:215
  77.4 0.0 collective-permute-done.refs_0_
  77.4 1.9 %collective-permute-start.2 = (f32[4096,128]{1,0:T(8,128)}, f32[4096,128]{1,0:T(8,128)}, u32[]{:S(2)}, u32[]{:S(2)}) collective-permute-start(f32[4096,128]{1,0:T(8,128)} %collective-permute-done.refs_0_), channel_id=1, source_target_pairs={{0,1},{1,0},{2,3},{3,2},{4,5},{5,4},{6,7},{7,6},{8,9},{9,8},{10,11... | collective-permute-start | bytes 6291464 | tf_op jit(solution)/shard_map/ppermute | solution.py:215
  79.4 0.7 reshape.18.idx_ref
  80.1 0.6 pad_add_fusion.place_ref
  80.7 0.0 all-to-all-done.refs_4_
  80.7 0.7 collective-permute-done.3.refs_3_
  81.3 3.2 %collective-permute-done.2.refs_2_ = f32[4096,128]{1,0:T(8,128)} collective-permute-done((f32[4096,128]{1,0:T(8,128)}, f32[4096,128]{1,0:T(8,128)}, u32[]{:S(2)}, u32[]{:S(2)}) %collective-permute-start.2) | collective-permute-done | bytes 2097184 | tf_op jit(solution)/shard_map/ppermute | solution.py:215
  84.5 6.4 %shard_map.59 = (f32[1024,128]{1,0:T(8,128)}, f32[128,128]{1,0:T(8,128)}) custom-call(s32[8,64]{1,0:T(8,128)} %reshape.18.idx_ref, s32[64]{0:T(128)} %count_ref.1, s32[2]{0:T(128)} %pad_add_fusion.place_ref, f32[8192,128]{1,0:T(8,128)} %own_ref.1, f32[4096,128]{1,0:T(8,128)} %collective-permute-done.refs_0_, f32[4096,128]{1,0:T(8,128)} %copy-done, ...), custom_call_target="tpu_custom_call" | custom-call | tf_op jit(solution)/shard_map/pallas_call | solution.py:106
  90.9 11.3 %all_to_all.20 = f32[32,4,128]{2,1,0:T(4,128)S(1)} all-to-all(f32[32,4,128]{2,1,0:T(4,128)} %bitcast.10), channel_id=1, replica_groups={{0,1,2,3,4,5,6,7,8,9,10,11,12,13,14,15,16,17,18,19,20,21,22,23,24,25,26..., dimensions={0} | all-to-all | bytes 131072 | tf_op jit(solution)/shard_map/all_to_all | solution.py:177
  102.3 24.0 %all_to_all.21 = f32[16,4,128]{2,1,0:T(4,128)S(1)} all-to-all(f32[16,4,128]{2,1,0:T(4,128)S(1)} %broadcast_in_dim.9), channel_id=1, replica_groups={{0,32,64,96,128,160,192,224,256,288,320,352,384,416,448,480},{1,33,65,9..., dimensions={0} | all-to-all | bytes 65536 | tf_op jit(solution)/shard_map/all_to_all | solution.py:177
  126.3 12.5 %all_to_all.22 = f32[32,4,128]{2,1,0:T(4,128)} all-to-all(f32[32,4,128]{2,1,0:T(4,128)S(1)} %broadcast_in_dim.18), channel_id=1, replica_groups={{0,1,2,3,4,5,6,7,8,9,10,11,12,13,14,15,16,17,18,19,20,21,22,23,24,25,26..., dimensions={0} | all-to-all | bytes 131072 | tf_op jit(solution)/shard_map/all_to_all | solution.py:177
  138.8 19.5 %shard_map.60 = (f32[1024,128]{1,0:T(8,128)}, f32[128,128]{1,0:T(8,128)}) custom-call(f32[128,128]{1,0:T(8,128)} %bitcast.9, f32[1024,128]{1,0:T(8,128)} %get-tuple-element.5.rows_ref), custom_call_target="tpu_custom_call" | custom-call | tf_op jit(solution)/shard_map/pallas_call | solution.py:160
  (6 shorter events, 0.1 us)
Async XLA Ops:
  5.1 67.0 %collective-permute-start.1 = (f32[4096,128]{1,0:T(8,128)}, f32[4096,128]{1,0:T(8,128)S(1)}, u32[]{:S(2)}, u32[]{:S(2)}) collective-permute-start(f32[4096,128]{1,0:T(8,128)} %get-tuple-element.6), channel_id=1, source_target_pairs={{0,8},{1,0},{2,10},{3,2},{4,12},{5,4},{6,14},{7,6},{8,16},{9,1},{1... | collective-permute-start | bytes 6291464 | tf_op jit(solution)/shard_map/ppermute | solution.py:210
  13.9 63.5 %collective-permute-start = (f32[4096,128]{1,0:T(8,128)}, f32[4096,128]{1,0:T(8,128)}, u32[]{:S(2)}, u32[]{:S(2)}) collective-permute-start(f32[4096,128]{1,0:T(8,128)} %get-tuple-element.7), channel_id=1, source_target_pairs={{0,8},{1,0},{2,10},{3,2},{4,12},{5,4},{6,14},{7,6},{8,16},{9,1},{1... | collective-permute-start | bytes 6291464 | tf_op jit(solution)/shard_map/ppermute | solution.py:210
  15.9 6.5 %copy-start.1 = (s32[64,1]{0,1:T(1,128)S(1)}, s32[64,1]{0,1:T(1,128)}, u32[]{:S(2)}) copy-start(s32[64,1]{0,1:T(1,128)} %param.6) | copy-start | bytes 772
  15.9 64.8 %all-to-all-start = ((f32[8,8,128,128]{3,2,1,0:T(8,128)}), f32[8,8,128,128]{3,2,1,0:T(8,128)}, u32[]{:S(2)}, u32[]{:S(2)}) async-start(f32[8,8,128,128]{3,2,1,0:T(8,128)} %bitcast.8), calls=%async_computation | async-start | bytes 8388608 | tf_op jit(solution)/shard_map/all_to_all | solution.py:216
  72.2 1.3 copy-start
  73.5 7.8 %collective-permute-start.3 = (f32[4096,128]{1,0:T(8,128)S(1)}, f32[4096,128]{1,0:T(8,128)}, u32[]{:S(2)}, u32[]{:S(2)}) collective-permute-start(f32[4096,128]{1,0:T(8,128)S(1)} %fusion.refs_1_), channel_id=1, source_target_pairs={{0,1},{1,0},{2,3},{3,2},{4,5},{5,4},{6,7},{7,6},{8,9},{9,8},{10,11... | collective-permute-start | bytes 6291464 | tf_op jit(solution)/shard_map/ppermute | solution.py:215
  77.4 7.1 %collective-permute-start.2 = (f32[4096,128]{1,0:T(8,128)}, f32[4096,128]{1,0:T(8,128)}, u32[]{:S(2)}, u32[]{:S(2)}) collective-permute-start(f32[4096,128]{1,0:T(8,128)} %collective-permute-done.refs_0_), channel_id=1, source_target_pairs={{0,1},{1,0},{2,3},{3,2},{4,5},{5,4},{6,7},{7,6},{8,9},{9,8},{10,11... | collective-permute-start | bytes 6291464 | tf_op jit(solution)/shard_map/ppermute | solution.py:215

commit v3 on v2

--- a/solution.py
+++ b/solution.py
@@ -20,30 +20,39 @@
 
 
 def product_kernel(
-    idx_ref, count_ref, place_ref, own_ref, *refs,
+    count_ref, own_ref, sent_ref, *refs,
 ):
     near_refs, far_refs = refs[:PARTS], refs[PARTS : 2 * PARTS]
-    tile_ref, out_ref, gram_ref, tile_buf, vec_buf, tile_sem, vec_sem = refs[2 * PARTS :]
-    slots, rows_kept, size, width = tile_ref.shape
+    out_ref, gram_ref, note_buf, tile_buf, vec_buf, note_sem, tile_sem, vec_sem = refs[2 * PARTS :]
+    slots = sent_ref.shape[0]
+    size, width = tile_buf.shape[2:]
+    rows_kept = out_ref.shape[0] // size
     blocks = own_ref.shape[0] // size
     part = blocks // PARTS
-    col, near_side = place_ref[0], place_ref[1]
-    first_row = col * rows_kept
 
     def copy_tiles(row):
-        return pltpu.make_async_copy(tile_ref.at[:, row], tile_buf.at[row], tile_sem.at[row])
+        start = pl.multiple_of(row * size, size)
+        return pltpu.make_async_copy(sent_ref.at[:, pl.ds(start, size)], tile_buf.at[row], tile_sem.at[row])
 
     def copy_vec(source, block, row, slot):
         start = pl.multiple_of(block * size, size)
         return pltpu.make_async_copy(source.at[pl.ds(start, size)], vec_buf.at[row, slot], vec_sem.at[row, slot])
 
+    notes = pltpu.make_async_copy(sent_ref.at[:, pl.ds(rows_kept * size, SUBLANES)], note_buf, note_sem)
+    notes.start()
+    copy_tiles(0).start()
+    notes.wait()
+    col = note_buf[0, 0, rows_kept].astype(jnp.int32)
+    first_row, near_side = col * rows_kept, 2 * (col % 2)
+
     def fetch(row, carry):
-        copy_tiles(row).start()
+        @pl.when(row > 0)
+        def _():
+            copy_tiles(row).start()
 
         def fetch_vec(slot, inner):
-            block = idx_ref[slot, first_row + row]
+            block = note_buf[slot, 0, row].astype(jnp.int32)
             side, within = block // blocks, block % blocks
-            number, place = within // part, within % part
 
             @pl.when(side == 1)
             def _():
@@ -51,6 +60,7 @@
 
             @pl.when(side != 1)
             def _():
+                number, place = within // part, within % part
                 for at in range(PARTS):
 
                     @pl.when((side == near_side) & (number == at))
@@ -98,9 +108,8 @@
     gram_ref[...] = gram[:width, :width] + (gram[:width, width:] + gram[width:, :width]) + gram[width:, width:]
 
 
-def product_and_gram(idx, counts, place, own, near, far, tiles):
-    slots, rows_kept, size, width = tiles.shape
-    in_smem = pl.BlockSpec(memory_space=pltpu.SMEM)
+def product_and_gram(counts, own, sent, near, far, rows_kept, size):
+    slots, width = sent.shape[0], own.shape[1]
     in_vmem = pl.BlockSpec(memory_space=pltpu.VMEM)
     anywhere = pl.BlockSpec(memory_space=pl.ANY)
     return pl.pallas_call(
@@ -109,16 +118,18 @@
             jax.ShapeDtypeStruct((rows_kept * size, width), jnp.float32),
             jax.ShapeDtypeStruct((width, width), jnp.float32),
         ),
-        in_specs=[in_smem] * 3 + [anywhere] * (2 + 2 * PARTS),
+        in_specs=[pl.BlockSpec(memory_space=pltpu.SMEM)] + [anywhere] * (2 + 2 * PARTS),
         out_specs=(in_vmem, in_vmem),
         scratch_shapes=[
+            pltpu.SMEM((slots, SUBLANES, width), jnp.float32),
             pltpu.VMEM((rows_kept, slots, size, size), jnp.float32),
             pltpu.VMEM((rows_kept, slots, size, width), jnp.float32),
+            pltpu.SemaphoreType.DMA,
             pltpu.SemaphoreType.DMA((rows_kept,)),
             pltpu.SemaphoreType.DMA((rows_kept, slots)),
         ],
         compiler_params=pltpu.CompilerParams(vmem_limit_bytes=62 << 20),
-    )(idx, counts, place, own, *near, *far, tiles)
+    )(counts, own, sent, *near, *far)
 
 
 def factor_kernel(nodes, gram_ref, rows_ref, basis_ref, factor_ref):
@@ -191,10 +202,9 @@
 def on_device(block_vector, op_tiles, tile_cols, live_counts):
     block_count, _, size, width = op_tiles.shape
     row_devices, col_devices = lax.axis_size("rows"), lax.axis_size("cols")
-    row, col = lax.axis_index("rows"), lax.axis_index("cols")
+    row = lax.axis_index("rows")
     rows_here = block_count * size
     rows_kept = block_count // col_devices
-    near_side = 2 * (col % 2)
 
     def fetched_by(r, c):
         if c % 2 == 0:
@@ -206,16 +216,19 @@
         to_r, to_c = fetched_by(r, c)
         steps.append((r * col_devices + c, to_r * col_devices + to_c))
     rows_part = rows_here // PARTS
-    near = [
-        lax.ppermute(block_vector[at * rows_part : (at + 1) * rows_part], ("rows", "cols"), steps) for at in range(PARTS)
-    ]
-    idx = lax.all_gather((tile_cols - (row - 1) * block_count).reshape(block_count), "cols")
-    head = jnp.where(jnp.min(idx) < 0, 0.0, near[-1][:SUBLANES])
-    near[-1] = lax.dynamic_update_slice(near[-1], head, (0, 0))
+    near = []
+    for at in range(PARTS):
+        source = lax.optimization_barrier(block_vector) if at else block_vector
+        near.append(lax.ppermute(source[at * rows_part : (at + 1) * rows_part], ("rows", "cols"), steps))
     far = [lax.ppermute(part, "cols", [(i, i ^ 1) for i in range(col_devices)]) for part in near]
-    tiles = lax.all_to_all(op_tiles.reshape(col_devices, rows_kept, size, size), "cols", 0, 0, tiled=True)
-    place = jnp.stack([col, near_side]).astype(jnp.int32)
-    part_rows, gram = product_and_gram(idx, live_counts, place, block_vector, near, far, tiles)
+
+    numbers = (tile_cols - (row - 1) * block_count).reshape(col_devices, rows_kept)
+    places = jnp.arange(col_devices, dtype=jnp.int32)[:, None]
+    note = jnp.concatenate([numbers, places], axis=1).astype(jnp.float32)
+    note = jnp.pad(note[:, None, :], ((0, 0), (0, SUBLANES - 1), (0, size - rows_kept - 1)))
+    sent = jnp.concatenate([op_tiles.reshape(col_devices, rows_kept * size, size), note], axis=1)
+    sent = lax.all_to_all(sent, "cols", 0, 0, tiled=True)
+    part_rows, gram = product_and_gram(live_counts, block_vector, sent, near, far, rows_kept, size)
     gram = sum_over_devices(gram, row_devices, col_devices)
     return basis_and_factor(rows_here * row_devices, gram, part_rows)
 

time: 159 us -> 150 us (0.943)
  blocking collectives: 96.2 us -> 48.3 us
  waiting for transfers between devices: 3.88 us -> 34.9 us
  starting transfers between devices: 21.1 us -> 28.2 us
  other arithmetic: 1.43 us -> 4.63 us
  local copies, waits for them, and re-layouts: 7.82 us -> 6.09 us
    unnamed x1 -> x0, blocking collectives: 48.4 us -> none
    ppermute x2, waiting for transfers between devices: 0.01 us -> 21.4 us  [on_device(): lax.ppermute(source[at * rows_part:(at + 1) * rows_part], ('rows', 'cols'...]
    all_to_all x1, waiting for transfers between devices: 0.01 us -> 13.5 us  [on_device(): sent = lax.all_to_all(sent, 'cols', 0, 0, tiled=True)]
    ppermute x2, starting transfers between devices: 5.83 us -> 13 us  [on_device(): lax.ppermute(part, 'cols', [(i, i ^ 1) for i in range(col_devices)])]
    concatenate x0 -> x1, other arithmetic: none -> 4.46 us  [on_device(): jnp.concatenate([op_tiles.reshape(col_devices, rows_kept * size, size), n...]
    ppermute x2, waiting for transfers between devices: 3.87 us -> 0.01 us  [on_device(): lax.ppermute(part, 'cols', [(i, i ^ 1) for i in range(col_devices)])]
    slice x1 -> x2, local copies, waits for them, and re-layouts: 4.51 us -> 4.65 us  [on_device(): source[at * rows_part:(at + 1) * rows_part]]
  transfers between devices with their start and end apart: 5 -> 5, of which waited for: 2 -> 3; matrix products, arithmetic and copies ran while one was open for 2% -> 4% of each run, Pallas kernels for 0% -> 0%
where the time goes in v3:
time: 150 us
  blocking collectives  48.3 us (32%)
  waiting for transfers between devices  34.9 us (23%)
  starting transfers between devices  28.2 us (19%)
  Pallas kernels  27 us (18%)
  local copies, waits for them, and re-layouts  6.09 us (4%)
  other arithmetic  4.63 us (3%)
    all_to_all x3, blocking collectives, exchange(): lax.all_to_all(pieces, ('rows', 'cols'), 0, 0, axis_index_groups=groups,...  48.3 us
    ppermute x2, waiting for transfers between devices, on_device(): lax.ppermute(source[at * rows_part:(at + 1) * rows_part], ('rows', 'cols'...  21.4 us
    pallas_call x1, Pallas kernels, basis_and_factor(): pl.pallas_call(functools.partial(factor_kernel, nodes), out_shape=(jax.Sh...  19.5 us
    all_to_all x1, waiting for transfers between devices, on_device(): sent = lax.all_to_all(sent, 'cols', 0, 0, tiled=True)  13.5 us
    ppermute x2, starting transfers between devices, on_device(): lax.ppermute(part, 'cols', [(i, i ^ 1) for i in range(col_devices)])  13 us
    ppermute x2, starting transfers between devices, on_device(): lax.ppermute(source[at * rows_part:(at + 1) * rows_part], ('rows', 'cols'...  10.7 us
    pallas_call x1, Pallas kernels, product_and_gram(): pl.pallas_call(product_kernel, out_shape=(jax.ShapeDtypeStruct((rows_kept...  7.49 us
    slice x2, local copies, waits for them, and re-layouts, on_device(): source[at * rows_part:(at + 1) * rows_part]  4.65 us
  transfers between devices with their start and end apart: 5, of which 3 were waited for; matrix products, arithmetic and copies ran while one was open for 4% of the time, Pallas kernels for 0%

profile of v3, /device:TPU:1, one launch (start us, length us, event | category | flops | bytes accessed | tf_op | source)
XLA Modules:
  0.0 149.8 jit_solution(9484603413680543638)
XLA Ops:
  0.6 0.0 copy-start
  0.6 0.0 copy-start.2
  0.7 3.2 %slice.6 = f32[4096,128]{1,0:T(8,128)} slice(f32[8192,128]{1,0:T(8,128)} %own_ref.1), slice={[0:4096], [0:128]} | slice | bytes 4194304 | tf_op jit(solution)/shard_map/slice | solution.py:222
  3.8 8.8 %collective-permute-start = (f32[4096,128]{1,0:T(8,128)}, f32[4096,128]{1,0:T(8,128)S(1)}, u32[]{:S(2)}, u32[]{:S(2)}) collective-permute-start(f32[4096,128]{1,0:T(8,128)} %slice.6), channel_id=1, source_target_pairs={{0,8},{1,0},{2,10},{3,2},{4,12},{5,4},{6,14},{7,6},{8,16},{9,1},{1... | collective-permute-start | bytes 6291464 | tf_op jit(solution)/shard_map/ppermute | solution.py:222
  12.6 0.0 copy-done
  12.6 1.5 slice.8
  14.1 1.9 %collective-permute-start.1 = (f32[4096,128]{1,0:T(8,128)}, f32[4096,128]{1,0:T(8,128)}, u32[]{:S(2)}, u32[]{:S(2)}) collective-permute-start(f32[4096,128]{1,0:T(8,128)} %slice.8), channel_id=1, source_target_pairs={{0,8},{1,0},{2,10},{3,2},{4,12},{5,4},{6,14},{7,6},{8,16},{9,1},{1... | collective-permute-start | bytes 6291464 | tf_op jit(solution)/shard_map/ppermute | solution.py:222
  16.0 0.0 copy-done.2
  16.1 0.1 concatenate.15
  16.1 0.1 add_convert_fusion
  16.2 4.5 %select_maximum_fusion = f32[8,1032,128]{2,1,0:T(8,128)} fusion(f32[8,1,9]{2,1,0:T(1,128)S(1)} %add_convert_fusion, f32[8,1024,128]{2,1,0:T(8,128)} %bitcast.4), kind=kLoop, calls=%fused_computation | loop fusion | flops 3170304 | bytes 8421664 | tf_op jit(solution)/shard_map/concatenate | solution.py:229
  20.7 4.5 %all-to-all-start = ((f32[8,1032,128]{2,1,0:T(8,128)}), f32[8,1032,128]{2,1,0:T(8,128)}, u32[]{:S(2)}, u32[]{:S(2)}) async-start(f32[8,1032,128]{2,1,0:T(8,128)} %select_maximum_fusion), calls=%async_computation | async-start | bytes 8454144 | tf_op jit(solution)/shard_map/all_to_all | solution.py:230
  25.2 6.7 %collective-permute-done.refs_0_ = f32[4096,128]{1,0:T(8,128)S(1)} collective-permute-done((f32[4096,128]{1,0:T(8,128)}, f32[4096,128]{1,0:T(8,128)S(1)}, u32[]{:S(2)}, u32[]{:S(2)}) %collective-permute-start) | collective-permute-done | bytes 2097184 | tf_op jit(solution)/shard_map/ppermute | solution.py:222
  31.9 0.0 copy-start.1
  31.9 1.3 copy-done.1
  33.2 6.5 %collective-permute-start.2 = (f32[4096,128]{1,0:T(8,128)S(1)}, f32[4096,128]{1,0:T(8,128)}, u32[]{:S(2)}, u32[]{:S(2)}) collective-permute-start(f32[4096,128]{1,0:T(8,128)S(1)} %collective-permute-done.refs_0_), channel_id=1, source_target_pairs={{0,1},{1,0},{2,3},{3,2},{4,5},{5,4},{6,7},{7,6},{8,9},{9,8},{10,11... | collective-permute-start | bytes 6291464 | tf_op jit(solution)/shard_map/ppermute | solution.py:223
  39.7 14.7 %collective-permute-done.1.refs_1_ = f32[4096,128]{1,0:T(8,128)} collective-permute-done((f32[4096,128]{1,0:T(8,128)}, f32[4096,128]{1,0:T(8,128)}, u32[]{:S(2)}, u32[]{:S(2)}) %collective-permute-start.1) | collective-permute-done | bytes 2097184 | tf_op jit(solution)/shard_map/ppermute | solution.py:222
  54.4 6.5 %collective-permute-start.3 = (f32[4096,128]{1,0:T(8,128)}, f32[4096,128]{1,0:T(8,128)}, u32[]{:S(2)}, u32[]{:S(2)}) collective-permute-start(f32[4096,128]{1,0:T(8,128)} %collective-permute-done.1.refs_1_), channel_id=1, source_target_pairs={{0,1},{1,0},{2,3},{3,2},{4,5},{5,4},{6,7},{7,6},{8,9},{9,8},{10,11... | collective-permute-start | bytes 6291464 | tf_op jit(solution)/shard_map/ppermute | solution.py:223
  60.9 13.5 %all-to-all-done.sent_ref = f32[8,1032,128]{2,1,0:T(8,128)} async-done(((f32[8,1032,128]{2,1,0:T(8,128)}), f32[8,1032,128]{2,1,0:T(8,128)}, u32[]{:S(2)}, u32[]{:S(2)}) %all-to-all-start) | async-done | bytes 4227104 | tf_op jit(solution)/shard_map/all_to_all | solution.py:230
  74.4 0.0 collective-permute-done.2.refs_2_
  74.4 0.0 collective-permute-done.3.refs_3_
  74.4 7.5 %shard_map.59 = (f32[1024,128]{1,0:T(8,128)}, f32[128,128]{1,0:T(8,128)}) custom-call(s32[64]{0:T(128)} %count_ref.1, f32[8192,128]{1,0:T(8,128)} %own_ref.1, f32[8,1032,128]{2,1,0:T(8,128)} %all-to-all-done.sent_ref, f32[4096,128]{1,0:T(8,128)} %copy-done.1, f32[4096,128]{1,0:T(8,128)} %collective-permute-done.1.refs_1_, ...), custom_call_target="tpu_custom_call" | custom-call | tf_op jit(solution)/shard_map/pallas_call | solution.py:115
  81.9 11.6 %all_to_all.20 = f32[32,4,128]{2,1,0:T(4,128)S(1)} all-to-all(f32[32,4,128]{2,1,0:T(4,128)} %bitcast.6), channel_id=1, replica_groups={{0,1,2,3,4,5,6,7,8,9,10,11,12,13,14,15,16,17,18,19,20,21,22,23,24,25,26..., dimensions={0} | all-to-all | bytes 131072 | tf_op jit(solution)/shard_map/all_to_all | solution.py:188
  93.6 24.2 %all_to_all.21 = f32[16,4,128]{2,1,0:T(4,128)S(1)} all-to-all(f32[16,4,128]{2,1,0:T(4,128)S(1)} %broadcast_in_dim.4), channel_id=1, replica_groups={{0,32,64,96,128,160,192,224,256,288,320,352,384,416,448,480},{1,33,65,9..., dimensions={0} | all-to-all | bytes 65536 | tf_op jit(solution)/shard_map/all_to_all | solution.py:188
  117.8 12.5 %all_to_all.22 = f32[32,4,128]{2,1,0:T(4,128)} all-to-all(f32[32,4,128]{2,1,0:T(4,128)S(1)} %broadcast_in_dim.5), channel_id=1, replica_groups={{0,1,2,3,4,5,6,7,8,9,10,11,12,13,14,15,16,17,18,19,20,21,22,23,24,25,26..., dimensions={0} | all-to-all | bytes 131072 | tf_op jit(solution)/shard_map/all_to_all | solution.py:188
  130.3 19.5 %shard_map.60 = (f32[1024,128]{1,0:T(8,128)}, f32[128,128]{1,0:T(8,128)}) custom-call(f32[128,128]{1,0:T(8,128)} %bitcast.5, f32[1024,128]{1,0:T(8,128)} %get-tuple-element.5.rows_ref), custom_call_target="tpu_custom_call" | custom-call | tf_op jit(solution)/shard_map/pallas_call | solution.py:171
  (6 shorter events, 0.1 us)
Async XLA Ops:
  0.6 12.0 %copy-start = (f32[8192,128]{1,0:T(8,128)S(1)}, f32[8192,128]{1,0:T(8,128)}, u32[]{:S(2)}) copy-start(f32[8192,128]{1,0:T(8,128)} %own_ref.1) | copy-start | bytes 12582916
  0.6 15.4 %copy-start.2 = (s32[64,1]{0,1:T(1,128)S(1)}, s32[64,1]{0,1:T(1,128)}, u32[]{:S(2)}) copy-start(s32[64,1]{0,1:T(1,128)} %param.6) | copy-start | bytes 772
  3.8 28.0 %collective-permute-start = (f32[4096,128]{1,0:T(8,128)}, f32[4096,128]{1,0:T(8,128)S(1)}, u32[]{:S(2)}, u32[]{:S(2)}) collective-permute-start(f32[4096,128]{1,0:T(8,128)} %slice.6), channel_id=1, source_target_pairs={{0,8},{1,0},{2,10},{3,2},{4,12},{5,4},{6,14},{7,6},{8,16},{9,1},{1... | collective-permute-start | bytes 6291464 | tf_op jit(solution)/shard_map/ppermute | solution.py:222
  14.1 40.3 %collective-permute-start.1 = (f32[4096,128]{1,0:T(8,128)}, f32[4096,128]{1,0:T(8,128)}, u32[]{:S(2)}, u32[]{:S(2)}) collective-permute-start(f32[4096,128]{1,0:T(8,128)} %slice.8), channel_id=1, source_target_pairs={{0,8},{1,0},{2,10},{3,2},{4,12},{5,4},{6,14},{7,6},{8,16},{9,1},{1... | collective-permute-start | bytes 6291464 | tf_op jit(solution)/shard_map/ppermute | solution.py:222
  20.7 53.7 %all-to-all-start = ((f32[8,1032,128]{2,1,0:T(8,128)}), f32[8,1032,128]{2,1,0:T(8,128)}, u32[]{:S(2)}, u32[]{:S(2)}) async-start(f32[8,1032,128]{2,1,0:T(8,128)} %select_maximum_fusion), calls=%async_computation | async-start | bytes 8454144 | tf_op jit(solution)/shard_map/all_to_all | solution.py:230
  31.9 1.3 copy-start.1
  33.2 41.2 %collective-permute-start.2 = (f32[4096,128]{1,0:T(8,128)S(1)}, f32[4096,128]{1,0:T(8,128)}, u32[]{:S(2)}, u32[]{:S(2)}) collective-permute-start(f32[4096,128]{1,0:T(8,128)S(1)} %collective-permute-done.refs_0_), channel_id=1, source_target_pairs={{0,1},{1,0},{2,3},{3,2},{4,5},{5,4},{6,7},{7,6},{8,9},{9,8},{10,11... | collective-permute-start | bytes 6291464 | tf_op jit(solution)/shard_map/ppermute | solution.py:223
  54.4 20.0 %collective-permute-start.3 = (f32[4096,128]{1,0:T(8,128)}, f32[4096,128]{1,0:T(8,128)}, u32[]{:S(2)}, u32[]{:S(2)}) collective-permute-start(f32[4096,128]{1,0:T(8,128)} %collective-permute-done.1.refs_1_), channel_id=1, source_target_pairs={{0,1},{1,0},{2,3},{3,2},{4,5},{5,4},{6,7},{7,6},{8,9},{9,8},{10,11... | collective-permute-start | bytes 6291464 | tf_op jit(solution)/shard_map/ppermute | solution.py:223

commit v4 on v3

--- a/solution.py
+++ b/solution.py
@@ -22,8 +22,8 @@
 def product_kernel(
     count_ref, own_ref, sent_ref, *refs,
 ):
-    near_refs, far_refs = refs[:PARTS], refs[PARTS : 2 * PARTS]
-    out_ref, gram_ref, note_buf, tile_buf, vec_buf, note_sem, tile_sem, vec_sem = refs[2 * PARTS :]
+    near_ref, far_refs = refs[0], refs[1 : 1 + PARTS]
+    out_ref, gram_ref, note_buf, tile_buf, vec_buf, note_sem, tile_sem, vec_sem = refs[1 + PARTS :]
     slots = sent_ref.shape[0]
     size, width = tile_buf.shape[2:]
     rows_kept = out_ref.shape[0] // size
@@ -58,18 +58,15 @@
             def _():
                 copy_vec(own_ref, within, row, slot).start()
 
-            @pl.when(side != 1)
+            @pl.when(side == near_side)
             def _():
-                number, place = within // part, within % part
-                for at in range(PARTS):
-
-                    @pl.when((side == near_side) & (number == at))
-                    def _():
-                        copy_vec(near_refs[at], place, row, slot).start()
-
-                    @pl.when((side != near_side) & (number == at))
-                    def _():
-                        copy_vec(far_refs[at], place, row, slot).start()
+                copy_vec(near_ref, within, row, slot).start()
+
+            for at in range(PARTS):
+
+                @pl.when((side != 1) & (side != near_side) & (within // part == at))
+                def _():
+                    copy_vec(far_refs[at], within % part, row, slot).start()
 
             return inner
 
@@ -118,7 +115,7 @@
             jax.ShapeDtypeStruct((rows_kept * size, width), jnp.float32),
             jax.ShapeDtypeStruct((width, width), jnp.float32),
         ),
-        in_specs=[pl.BlockSpec(memory_space=pltpu.SMEM)] + [anywhere] * (2 + 2 * PARTS),
+        in_specs=[pl.BlockSpec(memory_space=pltpu.SMEM)] + [anywhere] * (3 + PARTS),
         out_specs=(in_vmem, in_vmem),
         scratch_shapes=[
             pltpu.SMEM((slots, SUBLANES, width), jnp.float32),
@@ -129,37 +126,56 @@
             pltpu.SemaphoreType.DMA((rows_kept, slots)),
         ],
         compiler_params=pltpu.CompilerParams(vmem_limit_bytes=62 << 20),
-    )(counts, own, sent, *near, *far)
+    )(counts, own, sent, near, *far)
 
 
 def factor_kernel(nodes, gram_ref, rows_ref, basis_ref, factor_ref):
     size = gram_ref.shape[0]
     groups = size // SUBLANES
+    shape = (SUBLANES, size)
+    lane = lax.broadcasted_iota(jnp.int32, shape, 1)
+    sub = lax.broadcasted_iota(jnp.int32, shape, 0)
+    root = jnp.sqrt(jnp.float32(nodes))
+
+    def column(x, at):
+        return jnp.broadcast_to(x[:, at : at + 1], shape)
+
+    def line(x, at):
+        return jnp.broadcast_to(x[at : at + 1, :], shape)
+
+    def total(terms):
+        while len(terms) > 1:
+            terms = [terms[i] + terms[i + 1] for i in range(0, len(terms), 2)]
+        return terms[0]
+
     gram = [gram_ref[SUBLANES * i : SUBLANES * (i + 1), :] for i in range(groups)]
-    lane = lax.broadcasted_iota(jnp.int32, (SUBLANES, size), 1)
-    sub = lax.broadcasted_iota(jnp.int32, (SUBLANES, size), 0)
     inverse = [(lane == sub + SUBLANES * i).astype(jnp.float32) for i in range(groups)]
-    for step in range(size):
-        group, within = divmod(step, SUBLANES)
-        pivot_row = jnp.broadcast_to(gram[group][within : within + 1, :], (SUBLANES, size))
-        inverse_row = jnp.broadcast_to(inverse[group][within : within + 1, :], (SUBLANES, size))
-        scale = 1.0 / jnp.broadcast_to(pivot_row[:, step : step + 1], (SUBLANES, size))
-        pivot_row, inverse_row = pivot_row * scale, inverse_row * scale
-        for other in range(group, groups):
-            if other == group and within == SUBLANES - 1:
-                continue
-            factor = jnp.broadcast_to(gram[other][:, step : step + 1], (SUBLANES, size))
-            if other == group:
-                factor = jnp.where(sub > within, factor, 0.0)
-            gram[other] = gram[other] - factor * pivot_row
-            inverse[other] = inverse[other] - factor * inverse_row
-    root = jnp.sqrt(jnp.float32(nodes))
     for group in range(groups):
-        here = sub + SUBLANES * group
-        diagonal = jnp.sum(jnp.where(lane == here, gram[group], 0.0), axis=1, keepdims=True)
-        scale = lax.rsqrt(diagonal)
-        factor_ref[SUBLANES * group : SUBLANES * (group + 1), :] = jnp.where(lane >= here, gram[group] * scale, 0.0) / root
-        inverse[group] = inverse[group] * (scale * root)
+        first = SUBLANES * group
+        x, v = gram[group], inverse[group]
+        columns = [column(x, first + i) for i in range(SUBLANES)]
+        upper, solved, pivots = jnp.zeros(shape), jnp.zeros(shape), jnp.ones(shape)
+        for i in range(SUBLANES):
+            here = sub == i
+            pivot = line(columns[i], i)
+            scale = 1.0 / pivot
+            x_line, v_line = line(x, i), line(v, i)
+            upper, solved = jnp.where(here, x_line, upper), jnp.where(here, v_line, solved)
+            pivots = jnp.where(here, pivot, pivots)
+            weight = columns[i] * scale
+            x = jnp.where(here, x_line * scale, x - weight * x_line)
+            v = jnp.where(here, v_line * scale, v - weight * v_line)
+            for j in range(i + 1, SUBLANES):
+                c_line = line(columns[j], i)
+                columns[j] = jnp.where(here, c_line * scale, columns[j] - weight * c_line)
+        norm = lax.rsqrt(pivots)
+        factor_ref[first : first + SUBLANES, :] = jnp.where(lane >= sub + first, upper * norm, 0.0) / root
+        inverse[group] = solved * (norm * root)
+        x_lines, v_lines = [line(x, i) for i in range(SUBLANES)], [line(v, i) for i in range(SUBLANES)]
+        for below in range(group + 1, groups):
+            weights = [column(gram[below], first + i) for i in range(SUBLANES)]
+            gram[below] = gram[below] - total([weights[i] * x_lines[i] for i in range(SUBLANES)])
+            inverse[below] = inverse[below] - total([weights[i] * v_lines[i] for i in range(SUBLANES)])
     basis_ref[...] = lax.dot_general(
         rows_ref[...], jnp.concatenate(inverse, axis=0), (((1,), (1,)), ((), ())),
         precision=EXACT, preferred_element_type=jnp.float32,
@@ -216,11 +232,12 @@
         to_r, to_c = fetched_by(r, c)
         steps.append((r * col_devices + c, to_r * col_devices + to_c))
     rows_part = rows_here // PARTS
-    near = []
+    near = lax.ppermute(block_vector, ("rows", "cols"), steps)
+    far = []
     for at in range(PARTS):
-        source = lax.optimization_barrier(block_vector) if at else block_vector
-        near.append(lax.ppermute(source[at * rows_part : (at + 1) * rows_part], ("rows", "cols"), steps))
-    far = [lax.ppermute(part, "cols", [(i, i ^ 1) for i in range(col_devices)]) for part in near]
+        source = lax.optimization_barrier(near) if at else near
+        part = source[at * rows_part : (at + 1) * rows_part]
+        far.append(lax.ppermute(part, "cols", [(i, i ^ 1) for i in range(col_devices)]))
 
     numbers = (tile_cols - (row - 1) * block_count).reshape(col_devices, rows_kept)
     places = jnp.arange(col_devices, dtype=jnp.int32)[:, None]

time: 150 us -> 135 us (0.900)
  Pallas kernels: 27 us -> 14.2 us
  starting transfers between devices: 28.2 us -> 21.7 us
  blocking collectives: 48.3 us -> 51.3 us
  waiting for transfers between devices: 34.9 us -> 36.4 us
    pallas_call x1, Pallas kernels: 19.5 us -> 7.17 us  [basis_and_factor(): pl.pallas_call(functools.partial(factor_kernel, nodes), out_shape=(jax.Sh...]
    ppermute x2 -> x1, waiting for transfers between devices: 21.4 us -> 31.9 us  [on_device(): near = lax.ppermute(block_vector, ('rows', 'cols'), steps)]
    all_to_all x1, waiting for transfers between devices: 13.5 us -> 4.05 us  [on_device(): sent = lax.all_to_all(sent, 'cols', 0, 0, tiled=True)]
    ppermute x2, starting transfers between devices: 13 us -> 8.41 us  [on_device(): lax.ppermute(part, 'cols', [(i, i ^ 1) for i in range(col_devices)])]
    all_to_all x3, blocking collectives: 48.3 us -> 51.3 us  [exchange(): lax.all_to_all(pieces, ('rows', 'cols'), 0, 0, axis_index_groups=groups,...]
    ppermute x2 -> x1, starting transfers between devices: 10.7 us -> 8.79 us  [on_device(): near = lax.ppermute(block_vector, ('rows', 'cols'), steps)]
  transfers between devices with their start and end apart: 5 -> 4, of which waited for: 3 -> 3; matrix products, arithmetic and copies ran while one was open for 4% -> 7% of each run, Pallas kernels for 0% -> 0%
where the time goes in v4:
time: 135 us; the launch traced here: 134 us
  blocking collectives  51.3 us (38%)
  waiting for transfers between devices  36.4 us (27%)
  starting transfers between devices  21.7 us (16%)
  Pallas kernels  14.2 us (11%)
  other arithmetic  5.27 us (4%)
  local copies, waits for them, and re-layouts  4.89 us (4%)
    all_to_all x3, blocking collectives, exchange(): lax.all_to_all(pieces, ('rows', 'cols'), 0, 0, axis_index_groups=groups,...  51.3 us
    ppermute x1, waiting for transfers between devices, on_device(): near = lax.ppermute(block_vector, ('rows', 'cols'), steps)  31.9 us
    ppermute x1, starting transfers between devices, on_device(): near = lax.ppermute(block_vector, ('rows', 'cols'), steps)  8.79 us
    ppermute x2, starting transfers between devices, on_device(): lax.ppermute(part, 'cols', [(i, i ^ 1) for i in range(col_devices)])  8.41 us
    pallas_call x1, Pallas kernels, basis_and_factor(): pl.pallas_call(functools.partial(factor_kernel, nodes), out_shape=(jax.Sh...  7.17 us
    pallas_call x1, Pallas kernels, product_and_gram(): pl.pallas_call(product_kernel, out_shape=(jax.ShapeDtypeStruct((rows_kept...  7.01 us
    slice x2, local copies, waits for them, and re-layouts, on_device(): part = source[at * rows_part:(at + 1) * rows_part]  4.78 us
    all_to_all x1, starting transfers between devices, on_device(): sent = lax.all_to_all(sent, 'cols', 0, 0, tiled=True)  4.51 us
  transfers between devices with their start and end apart: 4, of which 3 were waited for; matrix products, arithmetic and copies ran while one was open for 7% of the time, Pallas kernels for 0%

profile of v4, /device:TPU:1, one launch (start us, length us, event | category | flops | bytes accessed | tf_op | source)
XLA Modules:
  0.0 134.4 jit_solution(1133994605431820595)
XLA Ops:
  0.6 8.8 %collective-permute-start = (f32[8192,128]{1,0:T(8,128)}, f32[8192,128]{1,0:T(8,128)}, u32[]{:S(2)}, u32[]{:S(2)}) collective-permute-start(f32[8192,128]{1,0:T(8,128)} %own_ref.1), channel_id=1, source_target_pairs={{0,8},{1,0},{2,10},{3,2},{4,12},{5,4},{6,14},{7,6},{8,16},{9,1},{1... | collective-permute-start | bytes 12582920 | tf_op jit(solution)/shard_map/ppermute | solution.py:235
  9.4 0.7 subtract_reduce_fusion
  10.1 0.1 concatenate.15
  10.2 0.1 add_convert_fusion
  10.3 4.4 %select_maximum_fusion = f32[8,1032,128]{2,1,0:T(8,128)} fusion(f32[8,1,9]{2,1,0:T(1,128)S(1)} %add_convert_fusion, f32[8,1024,128]{2,1,0:T(8,128)} %bitcast.4), kind=kLoop, calls=%fused_computation | loop fusion | flops 3170304 | bytes 8421664 | tf_op jit(solution)/shard_map/concatenate | solution.py:246
  14.7 4.5 %all-to-all-start = ((f32[8,1032,128]{2,1,0:T(8,128)}), f32[8,1032,128]{2,1,0:T(8,128)}, u32[]{:S(2)}, u32[]{:S(2)}) async-start(f32[8,1032,128]{2,1,0:T(8,128)} %select_maximum_fusion), calls=%async_computation | async-start | bytes 8454144 | tf_op jit(solution)/shard_map/all_to_all | solution.py:247
  19.2 31.9 %collective-permute-done.refs_0_ = f32[8192,128]{1,0:T(8,128)} collective-permute-done((f32[8192,128]{1,0:T(8,128)}, f32[8192,128]{1,0:T(8,128)}, u32[]{:S(2)}, u32[]{:S(2)}) %collective-permute-start) | collective-permute-done | bytes 4194336 | tf_op jit(solution)/shard_map/ppermute | solution.py:235
  51.2 1.7 %slice.8 = f32[4096,128]{1,0:T(8,128)S(1)} slice(f32[8192,128]{1,0:T(8,128)} %collective-permute-done.refs_0_), slice={[0:4096], [0:128]} | slice | bytes 4194304 | tf_op jit(solution)/shard_map/slice | solution.py:239
  52.9 6.5 %collective-permute-start.1 = (f32[4096,128]{1,0:T(8,128)S(1)}, f32[4096,128]{1,0:T(8,128)}, u32[]{:S(2)}, u32[]{:S(2)}) collective-permute-start(f32[4096,128]{1,0:T(8,128)S(1)} %slice.8), channel_id=1, source_target_pairs={{0,1},{1,0},{2,3},{3,2},{4,5},{5,4},{6,7},{7,6},{8,9},{9,8},{10,11... | collective-permute-start | bytes 6291464 | tf_op jit(solution)/shard_map/ppermute | solution.py:240
  59.4 3.1 %slice.9 = f32[4096,128]{1,0:T(8,128)} slice(f32[8192,128]{1,0:T(8,128)} %collective-permute-done.refs_0_), slice={[4096:8192], [0:128]} | slice | bytes 4194304 | tf_op jit(solution)/shard_map/slice | solution.py:239
  62.5 1.9 %collective-permute-start.2 = (f32[4096,128]{1,0:T(8,128)}, f32[4096,128]{1,0:T(8,128)}, u32[]{:S(2)}, u32[]{:S(2)}) collective-permute-start(f32[4096,128]{1,0:T(8,128)} %slice.9), channel_id=1, source_target_pairs={{0,1},{1,0},{2,3},{3,2},{4,5},{5,4},{6,7},{7,6},{8,9},{9,8},{10,11... | collective-permute-start | bytes 6291464 | tf_op jit(solution)/shard_map/ppermute | solution.py:240
  64.4 4.1 %all-to-all-done.sent_ref = f32[8,1032,128]{2,1,0:T(8,128)} async-done(((f32[8,1032,128]{2,1,0:T(8,128)}), f32[8,1032,128]{2,1,0:T(8,128)}, u32[]{:S(2)}, u32[]{:S(2)}) %all-to-all-start) | async-done | bytes 4227104 | tf_op jit(solution)/shard_map/all_to_all | solution.py:247
  68.4 0.0 collective-permute-done.1.refs_1_
  68.4 0.4 collective-permute-done.2.refs_2_
  68.8 7.0 %shard_map.59 = (f32[1024,128]{1,0:T(8,128)}, f32[128,128]{1,0:T(8,128)}) custom-call(s32[64]{0:T(128)} %count_ref.1, f32[8192,128]{1,0:T(8,128)} %own_ref.1, f32[8,1032,128]{2,1,0:T(8,128)} %all-to-all-done.sent_ref, f32[8192,128]{1,0:T(8,128)} %collective-permute-done.refs_0_, f32[4096,128]{1,0:T(8,128)} %collective-permute-done.1.refs_1_, ...), custom_call_target="tpu_custom_call" | custom-call | tf_op jit(solution)/shard_map/pallas_call | solution.py:112
  75.9 12.5 %all_to_all.20 = f32[32,4,128]{2,1,0:T(4,128)S(1)} all-to-all(f32[32,4,128]{2,1,0:T(4,128)} %bitcast.6), channel_id=1, replica_groups={{0,1,2,3,4,5,6,7,8,9,10,11,12,13,14,15,16,17,18,19,20,21,22,23,24,25,26..., dimensions={0} | all-to-all | bytes 131072 | tf_op jit(solution)/shard_map/all_to_all | solution.py:204
  88.4 26.2 %all_to_all.21 = f32[16,4,128]{2,1,0:T(4,128)S(1)} all-to-all(f32[16,4,128]{2,1,0:T(4,128)S(1)} %broadcast_in_dim.4), channel_id=1, replica_groups={{0,32,64,96,128,160,192,224,256,288,320,352,384,416,448,480},{1,33,65,9..., dimensions={0} | all-to-all | bytes 65536 | tf_op jit(solution)/shard_map/all_to_all | solution.py:204
  114.7 12.5 %all_to_all.22 = f32[32,4,128]{2,1,0:T(4,128)} all-to-all(f32[32,4,128]{2,1,0:T(4,128)S(1)} %broadcast_in_dim.5), channel_id=1, replica_groups={{0,1,2,3,4,5,6,7,8,9,10,11,12,13,14,15,16,17,18,19,20,21,22,23,24,25,26..., dimensions={0} | all-to-all | bytes 131072 | tf_op jit(solution)/shard_map/all_to_all | solution.py:204
  127.2 7.2 %shard_map.60 = (f32[1024,128]{1,0:T(8,128)}, f32[128,128]{1,0:T(8,128)}) custom-call(f32[128,128]{1,0:T(8,128)} %bitcast.5, f32[1024,128]{1,0:T(8,128)} %get-tuple-element.5.rows_ref), custom_call_target="tpu_custom_call" | custom-call | tf_op jit(solution)/shard_map/pallas_call | solution.py:187
  (5 shorter events, 0.1 us)
Async XLA Ops:
  0.6 50.5 %collective-permute-start = (f32[8192,128]{1,0:T(8,128)}, f32[8192,128]{1,0:T(8,128)}, u32[]{:S(2)}, u32[]{:S(2)}) collective-permute-start(f32[8192,128]{1,0:T(8,128)} %own_ref.1), channel_id=1, source_target_pairs={{0,8},{1,0},{2,10},{3,2},{4,12},{5,4},{6,14},{7,6},{8,16},{9,1},{1... | collective-permute-start | bytes 12582920 | tf_op jit(solution)/shard_map/ppermute | solution.py:235
  14.7 53.7 %all-to-all-start = ((f32[8,1032,128]{2,1,0:T(8,128)}), f32[8,1032,128]{2,1,0:T(8,128)}, u32[]{:S(2)}, u32[]{:S(2)}) async-start(f32[8,1032,128]{2,1,0:T(8,128)} %select_maximum_fusion), calls=%async_computation | async-start | bytes 8454144 | tf_op jit(solution)/shard_map/all_to_all | solution.py:247
  52.9 15.5 %collective-permute-start.1 = (f32[4096,128]{1,0:T(8,128)S(1)}, f32[4096,128]{1,0:T(8,128)}, u32[]{:S(2)}, u32[]{:S(2)}) collective-permute-start(f32[4096,128]{1,0:T(8,128)S(1)} %slice.8), channel_id=1, source_target_pairs={{0,1},{1,0},{2,3},{3,2},{4,5},{5,4},{6,7},{7,6},{8,9},{9,8},{10,11... | collective-permute-start | bytes 6291464 | tf_op jit(solution)/shard_map/ppermute | solution.py:240
  62.5 6.4 %collective-permute-start.2 = (f32[4096,128]{1,0:T(8,128)}, f32[4096,128]{1,0:T(8,128)}, u32[]{:S(2)}, u32[]{:S(2)}) collective-permute-start(f32[4096,128]{1,0:T(8,128)} %slice.9), channel_id=1, source_target_pairs={{0,1},{1,0},{2,3},{3,2},{4,5},{5,4},{6,7},{7,6},{8,9},{9,8},{10,11... | collective-permute-start | bytes 6291464 | tf_op jit(solution)/shard_map/ppermute | solution.py:240

commit v5 on v4

--- a/solution.py
+++ b/solution.py
@@ -10,6 +10,8 @@
 
 EXACT = lax.Precision.HIGHEST
 SUBLANES = 8
+PANEL = 2
+CHUNKS = 4
 PARTS = 2
 
 
@@ -19,9 +21,7 @@
     return high, low
 
 
-def product_kernel(
-    count_ref, own_ref, sent_ref, *refs,
-):
+def product_kernel(own_ref, sent_ref, *refs):
     near_ref, far_refs = refs[0], refs[1 : 1 + PARTS]
     out_ref, gram_ref, note_buf, tile_buf, vec_buf, note_sem, tile_sem, vec_sem = refs[1 + PARTS :]
     slots = sent_ref.shape[0]
@@ -38,12 +38,15 @@
         start = pl.multiple_of(block * size, size)
         return pltpu.make_async_copy(source.at[pl.ds(start, size)], vec_buf.at[row, slot], vec_sem.at[row, slot])
 
-    notes = pltpu.make_async_copy(sent_ref.at[:, pl.ds(rows_kept * size, SUBLANES)], note_buf, note_sem)
+    notes = pltpu.make_async_copy(sent_ref.at[:, pl.ds(rows_kept * size, 1)], note_buf, note_sem)
     notes.start()
     copy_tiles(0).start()
     notes.wait()
     col = note_buf[0, 0, rows_kept].astype(jnp.int32)
-    first_row, near_side = col * rows_kept, 2 * (col % 2)
+    near_side = 2 * (col % 2)
+
+    def count_of(row):
+        return note_buf[0, 0, rows_kept + 1 + row].astype(jnp.int32)
 
     def fetch(row, carry):
         @pl.when(row > 0)
@@ -52,7 +55,8 @@
 
         def fetch_vec(slot, inner):
             block = note_buf[slot, 0, row].astype(jnp.int32)
-            side, within = block // blocks, block % blocks
+            side = (block >= blocks).astype(jnp.int32) + (block >= 2 * blocks).astype(jnp.int32)
+            within = block - side * blocks
 
             @pl.when(side == 1)
             def _():
@@ -62,20 +66,22 @@
             def _():
                 copy_vec(near_ref, within, row, slot).start()
 
-            for at in range(PARTS):
-
-                @pl.when((side != 1) & (side != near_side) & (within // part == at))
-                def _():
-                    copy_vec(far_refs[at], within % part, row, slot).start()
+            @pl.when(side == 2 - near_side)
+            def _():
+                for at in range(PARTS):
+
+                    @pl.when((within >= at * part) & (within < (at + 1) * part))
+                    def _():
+                        copy_vec(far_refs[at], within - at * part, row, slot).start()
 
             return inner
 
-        return lax.fori_loop(0, count_ref[first_row + row], fetch_vec, carry)
+        return lax.fori_loop(0, count_of(row), fetch_vec, carry)
 
     lax.fori_loop(0, rows_kept, fetch, 0)
 
     def row_block(row, carry):
-        count = count_ref[first_row + row]
+        count = count_of(row)
         copy_tiles(row).wait()
 
         def wait_vec(slot, inner):
@@ -105,7 +111,7 @@
     gram_ref[...] = gram[:width, :width] + (gram[:width, width:] + gram[width:, :width]) + gram[width:, width:]
 
 
-def product_and_gram(counts, own, sent, near, far, rows_kept, size):
+def product_and_gram(own, sent, near, far, rows_kept, size):
     slots, width = sent.shape[0], own.shape[1]
     in_vmem = pl.BlockSpec(memory_space=pltpu.VMEM)
     anywhere = pl.BlockSpec(memory_space=pl.ANY)
@@ -115,10 +121,10 @@
             jax.ShapeDtypeStruct((rows_kept * size, width), jnp.float32),
             jax.ShapeDtypeStruct((width, width), jnp.float32),
         ),
-        in_specs=[pl.BlockSpec(memory_space=pltpu.SMEM)] + [anywhere] * (3 + PARTS),
+        in_specs=[anywhere] * (3 + PARTS),
         out_specs=(in_vmem, in_vmem),
         scratch_shapes=[
-            pltpu.SMEM((slots, SUBLANES, width), jnp.float32),
+            pltpu.SMEM((slots, 1, width), jnp.float32),
             pltpu.VMEM((rows_kept, slots, size, size), jnp.float32),
             pltpu.VMEM((rows_kept, slots, size, width), jnp.float32),
             pltpu.SemaphoreType.DMA,
@@ -126,16 +132,18 @@
             pltpu.SemaphoreType.DMA((rows_kept, slots)),
         ],
         compiler_params=pltpu.CompilerParams(vmem_limit_bytes=62 << 20),
-    )(counts, own, sent, near, *far)
-
-
-def factor_kernel(nodes, gram_ref, rows_ref, basis_ref, factor_ref):
+    )(own, sent, near, *far)
+
+
+def factor_kernel(nodes, gram_ref, rows_ref, basis_ref, factor_ref, rows_buf, basis_buf, rows_sem, basis_sem):
     size = gram_ref.shape[0]
     groups = size // SUBLANES
     shape = (SUBLANES, size)
     lane = lax.broadcasted_iota(jnp.int32, shape, 1)
     sub = lax.broadcasted_iota(jnp.int32, shape, 0)
     root = jnp.sqrt(jnp.float32(nodes))
+    bring = pltpu.make_async_copy(rows_ref, rows_buf, rows_sem)
+    bring.start()
 
     def column(x, at):
         return jnp.broadcast_to(x[:, at : at + 1], shape)
@@ -150,45 +158,70 @@
 
     gram = [gram_ref[SUBLANES * i : SUBLANES * (i + 1), :] for i in range(groups)]
     inverse = [(lane == sub + SUBLANES * i).astype(jnp.float32) for i in range(groups)]
-    for group in range(groups):
-        first = SUBLANES * group
-        x, v = gram[group], inverse[group]
-        columns = [column(x, first + i) for i in range(SUBLANES)]
-        upper, solved, pivots = jnp.zeros(shape), jnp.zeros(shape), jnp.ones(shape)
-        for i in range(SUBLANES):
-            here = sub == i
-            pivot = line(columns[i], i)
+    for start in range(0, groups, PANEL):
+        first = SUBLANES * start
+        height = SUBLANES * PANEL
+        rows = range(PANEL)
+        x, v = gram[start : start + PANEL], inverse[start : start + PANEL]
+        columns = [[column(x[q], first + i) for q in rows] for i in range(height)]
+        upper, solved, pivots = list(x), list(v), [jnp.ones(shape) for q in rows]
+        for i in range(height):
+            at, within = divmod(i, SUBLANES)
+            here = sub == within
+            pivot = line(columns[i][at], within)
+            x_line, v_line = line(x[at], within), line(v[at], within)
+            upper[at], solved[at] = jnp.where(here, x_line, upper[at]), jnp.where(here, v_line, solved[at])
+            pivots[at] = jnp.where(here, pivot, pivots[at])
             scale = 1.0 / pivot
-            x_line, v_line = line(x, i), line(v, i)
-            upper, solved = jnp.where(here, x_line, upper), jnp.where(here, v_line, solved)
-            pivots = jnp.where(here, pivot, pivots)
-            weight = columns[i] * scale
-            x = jnp.where(here, x_line * scale, x - weight * x_line)
-            v = jnp.where(here, v_line * scale, v - weight * v_line)
-            for j in range(i + 1, SUBLANES):
-                c_line = line(columns[j], i)
-                columns[j] = jnp.where(here, c_line * scale, columns[j] - weight * c_line)
-        norm = lax.rsqrt(pivots)
-        factor_ref[first : first + SUBLANES, :] = jnp.where(lane >= sub + first, upper * norm, 0.0) / root
-        inverse[group] = solved * (norm * root)
-        x_lines, v_lines = [line(x, i) for i in range(SUBLANES)], [line(v, i) for i in range(SUBLANES)]
-        for below in range(group + 1, groups):
-            weights = [column(gram[below], first + i) for i in range(SUBLANES)]
-            gram[below] = gram[below] - total([weights[i] * x_lines[i] for i in range(SUBLANES)])
-            inverse[below] = inverse[below] - total([weights[i] * v_lines[i] for i in range(SUBLANES)])
-    basis_ref[...] = lax.dot_general(
-        rows_ref[...], jnp.concatenate(inverse, axis=0), (((1,), (1,)), ((), ())),
-        precision=EXACT, preferred_element_type=jnp.float32,
-    )
+            weight = [columns[i][q] * scale for q in rows]
+            weight[at] = jnp.where(here, 0.0, weight[at])
+            for q in rows:
+                x[q], v[q] = x[q] - weight[q] * x_line, v[q] - weight[q] * v_line
+            for j in range(i + 1, height):
+                c_line = line(columns[j][at], within)
+                for q in rows:
+                    columns[j][q] = columns[j][q] - weight[q] * c_line
+        x_lines, v_lines = [], []
+        for q in rows:
+            scale, norm, begin = 1.0 / pivots[q], lax.rsqrt(pivots[q]), first + SUBLANES * q
+            factor_ref[begin : begin + SUBLANES, :] = jnp.where(lane >= sub + begin, upper[q] * norm, 0.0) / root
+            inverse[start + q] = solved[q] * (norm * root)
+            x[q], v[q] = x[q] * scale, v[q] * scale
+            x_lines += [line(x[q], i) for i in range(SUBLANES)]
+            v_lines += [line(v[q], i) for i in range(SUBLANES)]
+        for below in range(start + PANEL, groups):
+            weights = [column(gram[below], first + i) for i in range(height)]
+            gram[below] = gram[below] - total([weights[i] * x_lines[i] for i in range(height)])
+            inverse[below] = inverse[below] - total([weights[i] * v_lines[i] for i in range(height)])
+    solver = jnp.concatenate(inverse, axis=0)
+    bring.wait()
+    chunk = rows_buf.shape[0] // CHUNKS
+    copies = []
+    for at in range(CHUNKS):
+        here = pl.ds(at * chunk, chunk)
+        basis_buf[here, :] = lax.dot_general(
+            rows_buf[here, :], solver, (((1,), (1,)), ((), ())), precision=EXACT, preferred_element_type=jnp.float32
+        )
+        copies.append(pltpu.make_async_copy(basis_buf.at[here], basis_ref.at[here], basis_sem.at[at]))
+        copies[-1].start()
+    for copy in copies:
+        copy.wait()
 
 
 def basis_and_factor(nodes, gram, rows):
     in_vmem = pl.BlockSpec(memory_space=pltpu.VMEM)
+    in_hbm = pl.BlockSpec(memory_space=pltpu.HBM)
     return pl.pallas_call(
         functools.partial(factor_kernel, nodes),
         out_shape=(jax.ShapeDtypeStruct(rows.shape, jnp.float32), jax.ShapeDtypeStruct(gram.shape, jnp.float32)),
-        in_specs=[in_vmem] * 2,
-        out_specs=(in_vmem, in_vmem),
+        in_specs=[in_vmem, in_hbm],
+        out_specs=(in_hbm, in_vmem),
+        scratch_shapes=[
+            pltpu.VMEM(rows.shape, jnp.float32),
+            pltpu.VMEM(rows.shape, jnp.float32),
+            pltpu.SemaphoreType.DMA,
+            pltpu.SemaphoreType.DMA((CHUNKS,)),
+        ],
         compiler_params=pltpu.CompilerParams(vmem_limit_bytes=62 << 20),
     )(gram, rows)
 
@@ -241,11 +274,12 @@
 
     numbers = (tile_cols - (row - 1) * block_count).reshape(col_devices, rows_kept)
     places = jnp.arange(col_devices, dtype=jnp.int32)[:, None]
-    note = jnp.concatenate([numbers, places], axis=1).astype(jnp.float32)
-    note = jnp.pad(note[:, None, :], ((0, 0), (0, SUBLANES - 1), (0, size - rows_kept - 1)))
+    counts = live_counts.reshape(col_devices, rows_kept)
+    note = jnp.concatenate([numbers, places, counts], axis=1).astype(jnp.float32)
+    note = jnp.pad(note[:, None, :], ((0, 0), (0, SUBLANES - 1), (0, size - note.shape[1])))
     sent = jnp.concatenate([op_tiles.reshape(col_devices, rows_kept * size, size), note], axis=1)
     sent = lax.all_to_all(sent, "cols", 0, 0, tiled=True)
-    part_rows, gram = product_and_gram(live_counts, block_vector, sent, near, far, rows_kept, size)
+    part_rows, gram = product_and_gram(block_vector, sent, near, far, rows_kept, size)
     gram = sum_over_devices(gram, row_devices, col_devices)
     return basis_and_factor(rows_here * row_devices, gram, part_rows)
 

time: 135 us -> 134 us (level)
  Pallas kernels: 14.2 us -> 12.6 us
  transfers between devices with their start and end apart: 4 -> 4, of which waited for: 3 -> 2; matrix products, arithmetic and copies ran while one was open for 7% -> 8% of each run, Pallas kernels for 0% -> 0%
where the time goes in v5:
time: 134 us; the launch traced here: 133 us
  blocking collectives  51 us (38%)
  waiting for transfers between devices  36 us (27%)
  starting transfers between devices  21.7 us (16%)
  Pallas kernels  12.6 us (9%)
  local copies, waits for them, and re-layouts  5.62 us (4%)
  other arithmetic  5.28 us (4%)
    all_to_all x3, blocking collectives, exchange(): lax.all_to_all(pieces, ('rows', 'cols'), 0, 0, axis_index_groups=groups,...  51 us
    ppermute x1, waiting for transfers between devices, on_device(): near = lax.ppermute(block_vector, ('rows', 'cols'), steps)  31.2 us
    ppermute x1, starting transfers between devices, on_device(): near = lax.ppermute(block_vector, ('rows', 'cols'), steps)  8.79 us
    ppermute x2, starting transfers between devices, on_device(): lax.ppermute(part, 'cols', [(i, i ^ 1) for i in range(col_devices)])  8.41 us
    pallas_call x1, Pallas kernels, basis_and_factor(): pl.pallas_call(functools.partial(factor_kernel, nodes), out_shape=(jax.Sh...  6.86 us
    pallas_call x1, Pallas kernels, product_and_gram(): pl.pallas_call(product_kernel, out_shape=(jax.ShapeDtypeStruct((rows_kept...  5.75 us
    all_to_all x1, waiting for transfers between devices, on_device(): sent = lax.all_to_all(sent, 'cols', 0, 0, tiled=True)  4.8 us
    slice x2, local copies, waits for them, and re-layouts, on_device(): part = source[at * rows_part:(at + 1) * rows_part]  4.78 us
  transfers between devices with their start and end apart: 4, of which 2 were waited for; matrix products, arithmetic and copies ran while one was open for 8% of the time, Pallas kernels for 0%

profile of v5, /device:TPU:1, one launch (start us, length us, event | category | flops | bytes accessed | tf_op | source)
XLA Modules:
  0.0 132.9 jit_solution(8800536072543646027)
XLA Ops:
  0.6 8.8 %collective-permute-start = (f32[8192,128]{1,0:T(8,128)}, f32[8192,128]{1,0:T(8,128)}, u32[]{:S(2)}, u32[]{:S(2)}) collective-permute-start(f32[8192,128]{1,0:T(8,128)} %own_ref.1), channel_id=1, source_target_pairs={{0,8},{1,0},{2,10},{3,2},{4,12},{5,4},{6,14},{7,6},{8,16},{9,1},{1... | collective-permute-start | bytes 12582920 | tf_op jit(solution)/shard_map/ppermute | solution.py:268
  9.4 0.7 concatenate.18
  10.2 0.7 subtract_reduce_fusion
  10.8 0.1 concatenate.17
  10.9 0.1 add_convert_fusion
  11.0 4.4 %select_maximum_fusion = f32[8,1032,128]{2,1,0:T(8,128)} fusion(f32[8,1,17]{2,1,0:T(1,128)S(1)} %add_convert_fusion, f32[8,1024,128]{2,1,0:T(8,128)} %bitcast.5), kind=kLoop, calls=%fused_computation | loop fusion | flops 3170304 | bytes 8421920 | tf_op jit(solution)/shard_map/concatenate | solution.py:280
  15.5 4.5 %all-to-all-start = ((f32[8,1032,128]{2,1,0:T(8,128)}), f32[8,1032,128]{2,1,0:T(8,128)}, u32[]{:S(2)}, u32[]{:S(2)}) async-start(f32[8,1032,128]{2,1,0:T(8,128)} %select_maximum_fusion), calls=%async_computation | async-start | bytes 8454144 | tf_op jit(solution)/shard_map/all_to_all | solution.py:281
  20.0 31.2 %collective-permute-done.refs_0_ = f32[8192,128]{1,0:T(8,128)} collective-permute-done((f32[8192,128]{1,0:T(8,128)}, f32[8192,128]{1,0:T(8,128)}, u32[]{:S(2)}, u32[]{:S(2)}) %collective-permute-start) | collective-permute-done | bytes 4194336 | tf_op jit(solution)/shard_map/ppermute | solution.py:268
  51.2 1.7 %slice.8 = f32[4096,128]{1,0:T(8,128)S(1)} slice(f32[8192,128]{1,0:T(8,128)} %collective-permute-done.refs_0_), slice={[0:4096], [0:128]} | slice | bytes 4194304 | tf_op jit(solution)/shard_map/slice | solution.py:272
  52.9 6.5 %collective-permute-start.1 = (f32[4096,128]{1,0:T(8,128)S(1)}, f32[4096,128]{1,0:T(8,128)}, u32[]{:S(2)}, u32[]{:S(2)}) collective-permute-start(f32[4096,128]{1,0:T(8,128)S(1)} %slice.8), channel_id=1, source_target_pairs={{0,1},{1,0},{2,3},{3,2},{4,5},{5,4},{6,7},{7,6},{8,9},{9,8},{10,11... | collective-permute-start | bytes 6291464 | tf_op jit(solution)/shard_map/ppermute | solution.py:273
  59.4 3.1 %slice.9 = f32[4096,128]{1,0:T(8,128)} slice(f32[8192,128]{1,0:T(8,128)} %collective-permute-done.refs_0_), slice={[4096:8192], [0:128]} | slice | bytes 4194304 | tf_op jit(solution)/shard_map/slice | solution.py:272
  62.5 1.9 %collective-permute-start.2 = (f32[4096,128]{1,0:T(8,128)}, f32[4096,128]{1,0:T(8,128)}, u32[]{:S(2)}, u32[]{:S(2)}) collective-permute-start(f32[4096,128]{1,0:T(8,128)} %slice.9), channel_id=1, source_target_pairs={{0,1},{1,0},{2,3},{3,2},{4,5},{5,4},{6,7},{7,6},{8,9},{9,8},{10,11... | collective-permute-start | bytes 6291464 | tf_op jit(solution)/shard_map/ppermute | solution.py:273
  64.4 4.8 %all-to-all-done.sent_ref = f32[8,1032,128]{2,1,0:T(8,128)} async-done(((f32[8,1032,128]{2,1,0:T(8,128)}), f32[8,1032,128]{2,1,0:T(8,128)}, u32[]{:S(2)}, u32[]{:S(2)}) %all-to-all-start) | async-done | bytes 4227104 | tf_op jit(solution)/shard_map/all_to_all | solution.py:281
  69.2 0.0 collective-permute-done.1.refs_1_
  69.2 0.0 collective-permute-done.2.refs_2_
  69.2 5.7 %shard_map.59 = (f32[1024,128]{1,0:T(8,128)}, f32[128,128]{1,0:T(8,128)}) custom-call(f32[8192,128]{1,0:T(8,128)} %own_ref.1, f32[8,1032,128]{2,1,0:T(8,128)} %all-to-all-done.sent_ref, f32[8192,128]{1,0:T(8,128)} %collective-permute-done.refs_0_, f32[4096,128]{1,0:T(8,128)} %collective-permute-done.1.refs_1_, f32[4096,128]{1,0:T(8,128)} %collective-permute-done.2.refs_2_), custom_call_target="tpu_custom_call" | custom-call | tf_op jit(solution)/shard_map/pallas_call | solution.py:118
  74.9 12.5 %all_to_all.20 = f32[32,4,128]{2,1,0:T(4,128)S(1)} all-to-all(f32[32,4,128]{2,1,0:T(4,128)} %bitcast.7), channel_id=1, replica_groups={{0,1,2,3,4,5,6,7,8,9,10,11,12,13,14,15,16,17,18,19,20,21,22,23,24,25,26..., dimensions={0} | all-to-all | bytes 131072 | tf_op jit(solution)/shard_map/all_to_all | solution.py:237
  87.5 26.1 %all_to_all.21 = f32[16,4,128]{2,1,0:T(4,128)S(1)} all-to-all(f32[16,4,128]{2,1,0:T(4,128)S(1)} %broadcast_in_dim.4), channel_id=1, replica_groups={{0,32,64,96,128,160,192,224,256,288,320,352,384,416,448,480},{1,33,65,9..., dimensions={0} | all-to-all | bytes 65536 | tf_op jit(solution)/shard_map/all_to_all | solution.py:237
  113.6 12.5 %all_to_all.22 = f32[32,4,128]{2,1,0:T(4,128)} all-to-all(f32[32,4,128]{2,1,0:T(4,128)S(1)} %broadcast_in_dim.5), channel_id=1, replica_groups={{0,1,2,3,4,5,6,7,8,9,10,11,12,13,14,15,16,17,18,19,20,21,22,23,24,25,26..., dimensions={0} | all-to-all | bytes 131072 | tf_op jit(solution)/shard_map/all_to_all | solution.py:237
  126.1 6.9 %shard_map.60 = (f32[1024,128]{1,0:T(8,128)}, f32[128,128]{1,0:T(8,128)}) custom-call(f32[128,128]{1,0:T(8,128)} %bitcast.6, f32[1024,128]{1,0:T(8,128)} %get-tuple-element.5.rows_ref), custom_call_target="tpu_custom_call" | custom-call | tf_op jit(solution)/shard_map/pallas_call | solution.py:214
  (5 shorter events, 0.1 us)
Async XLA Ops:
  0.6 50.5 %collective-permute-start = (f32[8192,128]{1,0:T(8,128)}, f32[8192,128]{1,0:T(8,128)}, u32[]{:S(2)}, u32[]{:S(2)}) collective-permute-start(f32[8192,128]{1,0:T(8,128)} %own_ref.1), channel_id=1, source_target_pairs={{0,8},{1,0},{2,10},{3,2},{4,12},{5,4},{6,14},{7,6},{8,16},{9,1},{1... | collective-permute-start | bytes 12582920 | tf_op jit(solution)/shard_map/ppermute | solution.py:268
  15.5 53.7 %all-to-all-start = ((f32[8,1032,128]{2,1,0:T(8,128)}), f32[8,1032,128]{2,1,0:T(8,128)}, u32[]{:S(2)}, u32[]{:S(2)}) async-start(f32[8,1032,128]{2,1,0:T(8,128)} %select_maximum_fusion), calls=%async_computation | async-start | bytes 8454144 | tf_op jit(solution)/shard_map/all_to_all | solution.py:281
  52.9 16.3 %collective-permute-start.1 = (f32[4096,128]{1,0:T(8,128)S(1)}, f32[4096,128]{1,0:T(8,128)}, u32[]{:S(2)}, u32[]{:S(2)}) collective-permute-start(f32[4096,128]{1,0:T(8,128)S(1)} %slice.8), channel_id=1, source_target_pairs={{0,1},{1,0},{2,3},{3,2},{4,5},{5,4},{6,7},{7,6},{8,9},{9,8},{10,11... | collective-permute-start | bytes 6291464 | tf_op jit(solution)/shard_map/ppermute | solution.py:273
  62.5 6.7 %collective-permute-start.2 = (f32[4096,128]{1,0:T(8,128)}, f32[4096,128]{1,0:T(8,128)}, u32[]{:S(2)}, u32[]{:S(2)}) collective-permute-start(f32[4096,128]{1,0:T(8,128)} %slice.9), channel_id=1, source_target_pairs={{0,1},{1,0},{2,3},{3,2},{4,5},{5,4},{6,7},{7,6},{8,9},{9,8},{10,11... | collective-permute-start | bytes 6291464 | tf_op jit(solution)/shard_map/ppermute | solution.py:273

commit v6 on v5

--- a/solution.py
+++ b/solution.py
@@ -12,7 +12,6 @@
 SUBLANES = 8
 PANEL = 2
 CHUNKS = 4
-PARTS = 2
 
 
 def split_bf16(x):
@@ -21,14 +20,13 @@
     return high, low
 
 
-def product_kernel(own_ref, sent_ref, *refs):
-    near_ref, far_refs = refs[0], refs[1 : 1 + PARTS]
-    out_ref, gram_ref, note_buf, tile_buf, vec_buf, note_sem, tile_sem, vec_sem = refs[1 + PARTS :]
+def product_kernel(
+    table_ref, own_ref, sent_ref, near_ref, far_ref, out_ref, gram_ref, tile_buf, vec_buf, tile_sem, vec_sem
+):
     slots = sent_ref.shape[0]
     size, width = tile_buf.shape[2:]
     rows_kept = out_ref.shape[0] // size
     blocks = own_ref.shape[0] // size
-    part = blocks // PARTS
 
     def copy_tiles(row):
         start = pl.multiple_of(row * size, size)
@@ -38,15 +36,11 @@
         start = pl.multiple_of(block * size, size)
         return pltpu.make_async_copy(source.at[pl.ds(start, size)], vec_buf.at[row, slot], vec_sem.at[row, slot])
 
-    notes = pltpu.make_async_copy(sent_ref.at[:, pl.ds(rows_kept * size, 1)], note_buf, note_sem)
-    notes.start()
     copy_tiles(0).start()
-    notes.wait()
-    col = note_buf[0, 0, rows_kept].astype(jnp.int32)
-    near_side = 2 * (col % 2)
+    kept_from, near_side = table_ref[slots + 1, 0] * rows_kept, table_ref[slots + 1, 1]
 
     def count_of(row):
-        return note_buf[0, 0, rows_kept + 1 + row].astype(jnp.int32)
+        return table_ref[slots, kept_from + row]
 
     def fetch(row, carry):
         @pl.when(row > 0)
@@ -54,7 +48,7 @@
             copy_tiles(row).start()
 
         def fetch_vec(slot, inner):
-            block = note_buf[slot, 0, row].astype(jnp.int32)
+            block = table_ref[slot, kept_from + row]
             side = (block >= blocks).astype(jnp.int32) + (block >= 2 * blocks).astype(jnp.int32)
             within = block - side * blocks
 
@@ -68,11 +62,7 @@
 
             @pl.when(side == 2 - near_side)
             def _():
-                for at in range(PARTS):
-
-                    @pl.when((within >= at * part) & (within < (at + 1) * part))
-                    def _():
-                        copy_vec(far_refs[at], within - at * part, row, slot).start()
+                copy_vec(far_ref, within, row, slot).start()
 
             return inner
 
@@ -111,7 +101,34 @@
     gram_ref[...] = gram[:width, :width] + (gram[:width, width:] + gram[width:, :width]) + gram[width:, width:]
 
 
-def product_and_gram(own, sent, near, far, rows_kept, size):
+def decode_kernel(first, count_ref, sent_ref, table_ref, note_buf, sem):
+    notes = pltpu.make_async_copy(sent_ref.at[:, pl.ds(first, SUBLANES)], note_buf, sem)
+    notes.start()
+    slots = note_buf.shape[0]
+    blocks = count_ref.shape[1]
+    row, col = lax.axis_index("rows"), lax.axis_index("cols")
+    table_ref[slots : slots + 1, :blocks] = count_ref[...]
+    at = lax.broadcasted_iota(jnp.int32, (1, table_ref.shape[1]), 1)
+    table_ref[slots + 1 : slots + 2, :] = jnp.where(at == 0, col, 2 * (col % 2))
+    notes.wait()
+    for slot in range(slots):
+        table_ref[slot : slot + 1, :] = note_buf[slot, 0:1, :].astype(jnp.int32) - (row - 1) * blocks
+
+
+def decode(counts, sent, first):
+    slots, _, size = sent.shape
+    return pl.pallas_call(
+        functools.partial(decode_kernel, first),
+        out_shape=jax.ShapeDtypeStruct((slots + SUBLANES, size), jnp.int32),
+        in_specs=[pl.BlockSpec(memory_space=pltpu.VMEM), pl.BlockSpec(memory_space=pl.ANY)],
+        out_specs=pl.BlockSpec(memory_space=pltpu.VMEM),
+        scratch_shapes=[pltpu.VMEM((slots, SUBLANES, size), jnp.float32), pltpu.SemaphoreType.DMA],
+        compiler_params=pltpu.CompilerParams(vmem_limit_bytes=62 << 20),
+        cost_estimate=pl.CostEstimate(flops=1 << 33, bytes_accessed=1 << 26, transcendentals=0),
+    )(counts, sent)
+
+
+def product_and_gram(table, own, sent, near, far, rows_kept, size):
     slots, width = sent.shape[0], own.shape[1]
     in_vmem = pl.BlockSpec(memory_space=pltpu.VMEM)
     anywhere = pl.BlockSpec(memory_space=pl.ANY)
@@ -121,18 +138,16 @@
             jax.ShapeDtypeStruct((rows_kept * size, width), jnp.float32),
             jax.ShapeDtypeStruct((width, width), jnp.float32),
         ),
-        in_specs=[anywhere] * (3 + PARTS),
+        in_specs=[pl.BlockSpec(memory_space=pltpu.SMEM)] + [anywhere] * 4,
         out_specs=(in_vmem, in_vmem),
         scratch_shapes=[
-            pltpu.SMEM((slots, 1, width), jnp.float32),
             pltpu.VMEM((rows_kept, slots, size, size), jnp.float32),
             pltpu.VMEM((rows_kept, slots, size, width), jnp.float32),
-            pltpu.SemaphoreType.DMA,
             pltpu.SemaphoreType.DMA((rows_kept,)),
             pltpu.SemaphoreType.DMA((rows_kept, slots)),
         ],
         compiler_params=pltpu.CompilerParams(vmem_limit_bytes=62 << 20),
-    )(own, sent, near, *far)
+    )(table, own, sent, near, far)
 
 
 def factor_kernel(nodes, gram_ref, rows_ref, basis_ref, factor_ref, rows_buf, basis_buf, rows_sem, basis_sem):
@@ -216,13 +231,14 @@
         out_shape=(jax.ShapeDtypeStruct(rows.shape, jnp.float32), jax.ShapeDtypeStruct(gram.shape, jnp.float32)),
         in_specs=[in_vmem, in_hbm],
         out_specs=(in_hbm, in_vmem),
+        input_output_aliases={1: 0},
         scratch_shapes=[
             pltpu.VMEM(rows.shape, jnp.float32),
             pltpu.VMEM(rows.shape, jnp.float32),
             pltpu.SemaphoreType.DMA,
             pltpu.SemaphoreType.DMA((CHUNKS,)),
         ],
-        compiler_params=pltpu.CompilerParams(vmem_limit_bytes=62 << 20),
+        compiler_params=pltpu.CompilerParams(vmem_limit_bytes=16 << 20),
     )(gram, rows)
 
 
@@ -251,7 +267,6 @@
 def on_device(block_vector, op_tiles, tile_cols, live_counts):
     block_count, _, size, width = op_tiles.shape
     row_devices, col_devices = lax.axis_size("rows"), lax.axis_size("cols")
-    row = lax.axis_index("rows")
     rows_here = block_count * size
     rows_kept = block_count // col_devices
 
@@ -264,22 +279,15 @@
     for r, c in itertools.product(range(row_devices), range(col_devices)):
         to_r, to_c = fetched_by(r, c)
         steps.append((r * col_devices + c, to_r * col_devices + to_c))
-    rows_part = rows_here // PARTS
     near = lax.ppermute(block_vector, ("rows", "cols"), steps)
-    far = []
-    for at in range(PARTS):
-        source = lax.optimization_barrier(near) if at else near
-        part = source[at * rows_part : (at + 1) * rows_part]
-        far.append(lax.ppermute(part, "cols", [(i, i ^ 1) for i in range(col_devices)]))
-
-    numbers = (tile_cols - (row - 1) * block_count).reshape(col_devices, rows_kept)
-    places = jnp.arange(col_devices, dtype=jnp.int32)[:, None]
-    counts = live_counts.reshape(col_devices, rows_kept)
-    note = jnp.concatenate([numbers, places, counts], axis=1).astype(jnp.float32)
-    note = jnp.pad(note[:, None, :], ((0, 0), (0, SUBLANES - 1), (0, size - note.shape[1])))
+    far = lax.ppermute(near, "cols", [(i, i ^ 1) for i in range(col_devices)])
+
+    note = jnp.pad(tile_cols.reshape(1, 1, block_count).astype(jnp.float32), ((0, 0), (0, 0), (0, size - block_count)))
+    note = jnp.broadcast_to(note, (col_devices, SUBLANES, size))
     sent = jnp.concatenate([op_tiles.reshape(col_devices, rows_kept * size, size), note], axis=1)
     sent = lax.all_to_all(sent, "cols", 0, 0, tiled=True)
-    part_rows, gram = product_and_gram(block_vector, sent, near, far, rows_kept, size)
+    table = decode(live_counts.reshape(1, block_count), sent, rows_kept * size)
+    part_rows, gram = product_and_gram(table, block_vector, sent, near, far, rows_kept, size)
     gram = sum_over_devices(gram, row_devices, col_devices)
     return basis_and_factor(rows_here * row_devices, gram, part_rows)
 

time: 134 us -> 131 us (0.978)
  waiting for transfers between devices: 36 us -> 42.7 us
  local copies, waits for them, and re-layouts: 5.62 us -> 0.04 us
  blocking collectives: 51 us -> 47.4 us
  Pallas kernels: 12.6 us -> 14.6 us
  starting transfers between devices: 21.7 us -> 19.8 us
    all_to_all x1, waiting for transfers between devices: 4.8 us -> 10.6 us  [on_device(): sent = lax.all_to_all(sent, 'cols', 0, 0, tiled=True)]
    slice x2 -> x0, local copies, waits for them, and re-layouts: 4.78 us -> none  [on_device(): part = source[at * rows_part:(at + 1) * rows_part]]
    all_to_all x3, blocking collectives: 51 us -> 47.4 us  [exchange(): lax.all_to_all(pieces, ('rows', 'cols'), 0, 0, axis_index_groups=groups,...]
    pallas_call x0 -> x1, Pallas kernels: none -> 2.02 us  [decode(): pl.pallas_call(functools.partial(decode_kernel, first), out_shape=jax.Sha...]
    ppermute x2 -> x1, starting transfers between devices: 8.41 us -> 6.49 us  [on_device(): far = lax.ppermute(near, 'cols', [(i, i ^ 1) for i in range(col_devices)])]
  transfers between devices with their start and end apart: 4 -> 3, of which waited for: 2 -> 2; matrix products, arithmetic and copies ran while one was open for 8% -> 4% of each run, Pallas kernels for 0% -> 2%
where the time goes in v6:
time: 131 us; the launch traced here: 130 us
  blocking collectives  47.4 us (36%)
  waiting for transfers between devices  42.7 us (33%)
  starting transfers between devices  19.8 us (15%)
  Pallas kernels  14.6 us (11%)
  other arithmetic  5.17 us (4%)
    all_to_all x3, blocking collectives, exchange(): lax.all_to_all(pieces, ('rows', 'cols'), 0, 0, axis_index_groups=groups,...  47.4 us
    ppermute x1, waiting for transfers between devices, on_device(): near = lax.ppermute(block_vector, ('rows', 'cols'), steps)  32.1 us
    all_to_all x1, waiting for transfers between devices, on_device(): sent = lax.all_to_all(sent, 'cols', 0, 0, tiled=True)  10.6 us
    ppermute x1, starting transfers between devices, on_device(): near = lax.ppermute(block_vector, ('rows', 'cols'), steps)  8.79 us
    pallas_call x1, Pallas kernels, product_and_gram(): pl.pallas_call(product_kernel, out_shape=(jax.ShapeDtypeStruct((rows_kept...  6.53 us
    ppermute x1, starting transfers between devices, on_device(): far = lax.ppermute(near, 'cols', [(i, i ^ 1) for i in range(col_devices)])  6.49 us
    pallas_call x1, Pallas kernels, basis_and_factor(): pl.pallas_call(functools.partial(factor_kernel, nodes), out_shape=(jax.Sh...  6.02 us
    all_to_all x1, starting transfers between devices, on_device(): sent = lax.all_to_all(sent, 'cols', 0, 0, tiled=True)  4.51 us
  transfers between devices with their start and end apart: 3, of which 2 were waited for; matrix products, arithmetic and copies ran while one was open for 4% of the time, Pallas kernels for 2%

profile of v6, /device:TPU:1, one launch (start us, length us, event | category | flops | bytes accessed | tf_op | source)
XLA Modules:
  0.0 130.3 jit_solution(1078576027389754511)
XLA Ops:
  0.6 8.8 %collective-permute-start = (f32[8192,128]{1,0:T(8,128)}, f32[8192,128]{1,0:T(8,128)}, u32[]{:S(2)}, u32[]{:S(2)}) collective-permute-start(f32[8192,128]{1,0:T(8,128)} %own_ref.1), channel_id=1, source_target_pairs={{0,8},{1,0},{2,10},{3,2},{4,12},{5,4},{6,14},{7,6},{8,16},{9,1},{1... | collective-permute-start | bytes 12582920 | tf_op jit(solution)/shard_map/ppermute | solution.py:282
  9.4 0.7 convert_bitcast_fusion
  10.1 4.4 %pad_maximum_fusion = f32[8,1032,128]{2,1,0:T(8,128)} fusion(f32[8,8,128]{2,1,0:T(8,128)S(1)} %broadcast_in_dim.9, f32[8,1024,128]{2,1,0:T(8,128)} %bitcast.9), kind=kLoop, calls=%fused_computation | loop fusion | flops 1056768 | bytes 8454144 | tf_op jit(solution)/shard_map/concatenate | solution.py:287
  14.5 4.5 %all-to-all-start = ((f32[8,1032,128]{2,1,0:T(8,128)}), f32[8,1032,128]{2,1,0:T(8,128)}, u32[]{:S(2)}, u32[]{:S(2)}) async-start(f32[8,1032,128]{2,1,0:T(8,128)} %pad_maximum_fusion), calls=%async_computation | async-start | bytes 8454144 | tf_op jit(solution)/shard_map/all_to_all | solution.py:288
  19.1 32.1 %collective-permute-done.near_ref = f32[8192,128]{1,0:T(8,128)} collective-permute-done((f32[8192,128]{1,0:T(8,128)}, f32[8192,128]{1,0:T(8,128)}, u32[]{:S(2)}, u32[]{:S(2)}) %collective-permute-start) | collective-permute-done | bytes 4194336 | tf_op jit(solution)/shard_map/ppermute | solution.py:282
  51.2 6.5 %collective-permute-start.1 = (f32[8192,128]{1,0:T(8,128)}, f32[8192,128]{1,0:T(8,128)}, u32[]{:S(2)}, u32[]{:S(2)}) collective-permute-start(f32[8192,128]{1,0:T(8,128)} %collective-permute-done.near_ref), channel_id=1, source_target_pairs={{0,1},{1,0},{2,3},{3,2},{4,5},{5,4},{6,7},{7,6},{8,9},{9,8},{10,11... | collective-permute-start | bytes 12582920 | tf_op jit(solution)/shard_map/ppermute | solution.py:283
  57.7 10.6 %all-to-all-done.sent_ref = f32[8,1032,128]{2,1,0:T(8,128)} async-done(((f32[8,1032,128]{2,1,0:T(8,128)}), f32[8,1032,128]{2,1,0:T(8,128)}, u32[]{:S(2)}, u32[]{:S(2)}) %all-to-all-start) | async-done | bytes 4227104 | tf_op jit(solution)/shard_map/all_to_all | solution.py:288
  68.3 2.0 %shard_map.59.table_ref = s32[16,128]{1,0:T(8,128)} custom-call(s32[1,64]{1,0:T(1,128)} %bitcast.11, f32[8,1032,128]{2,1,0:T(8,128)} %all-to-all-done.sent_ref), custom_call_target="tpu_custom_call" | custom-call | flops 8589934592 | bytes 67108864 | tf_op jit(solution)/shard_map/pallas_call | solution.py:120
  70.3 0.0 collective-permute-done.1.far_ref
  70.3 6.5 %shard_map.60 = (f32[1024,128]{1,0:T(8,128)}, f32[128,128]{1,0:T(8,128)}) custom-call(s32[16,128]{1,0:T(8,128)} %shard_map.59.table_ref, f32[8192,128]{1,0:T(8,128)} %own_ref.1, f32[8,1032,128]{2,1,0:T(8,128)} %all-to-all-done.sent_ref, f32[8192,128]{1,0:T(8,128)} %collective-permute-done.near_ref, f32[8192,128]{1,0:T(8,128)} %collective-permute-done.1.far_ref), custom_call_target="tpu_custom_call" | custom-call | tf_op jit(solution)/shard_map/pallas_call | solution.py:135
  76.8 11.8 %all_to_all.20 = f32[32,4,128]{2,1,0:T(4,128)S(1)} all-to-all(f32[32,4,128]{2,1,0:T(4,128)} %bitcast.10), channel_id=1, replica_groups={{0,1,2,3,4,5,6,7,8,9,10,11,12,13,14,15,16,17,18,19,20,21,22,23,24,25,26..., dimensions={0} | all-to-all | bytes 131072 | tf_op jit(solution)/shard_map/all_to_all | solution.py:253
  88.6 23.3 %all_to_all.21 = f32[16,4,128]{2,1,0:T(4,128)S(1)} all-to-all(f32[16,4,128]{2,1,0:T(4,128)S(1)} %broadcast_in_dim.10), channel_id=1, replica_groups={{0,32,64,96,128,160,192,224,256,288,320,352,384,416,448,480},{1,33,65,9..., dimensions={0} | all-to-all | bytes 65536 | tf_op jit(solution)/shard_map/all_to_all | solution.py:253
  112.0 12.3 %all_to_all.22 = f32[32,4,128]{2,1,0:T(4,128)S(1)} all-to-all(f32[32,4,128]{2,1,0:T(4,128)S(1)} %broadcast_in_dim.22), channel_id=1, replica_groups={{0,1,2,3,4,5,6,7,8,9,10,11,12,13,14,15,16,17,18,19,20,21,22,23,24,25,26..., dimensions={0} | all-to-all | bytes 131072 | tf_op jit(solution)/shard_map/all_to_all | solution.py:253
  124.3 6.0 %shard_map.61 = (f32[1024,128]{1,0:T(8,128)}, f32[128,128]{1,0:T(8,128)}) custom-call(f32[128,128]{1,0:T(8,128)S(1)} %bitcast.8, f32[1024,128]{1,0:T(8,128)} %get-tuple-element.5.rows_ref), custom_call_target="tpu_custom_call", output_to_operand_aliasing={{0}: (1, {})} | custom-call | tf_op jit(solution)/shard_map/pallas_call | solution.py:229
  (6 shorter events, 0.1 us)
Async XLA Ops:
  0.6 50.5 %collective-permute-start = (f32[8192,128]{1,0:T(8,128)}, f32[8192,128]{1,0:T(8,128)}, u32[]{:S(2)}, u32[]{:S(2)}) collective-permute-start(f32[8192,128]{1,0:T(8,128)} %own_ref.1), channel_id=1, source_target_pairs={{0,8},{1,0},{2,10},{3,2},{4,12},{5,4},{6,14},{7,6},{8,16},{9,1},{1... | collective-permute-start | bytes 12582920 | tf_op jit(solution)/shard_map/ppermute | solution.py:282
  14.5 53.7 %all-to-all-start = ((f32[8,1032,128]{2,1,0:T(8,128)}), f32[8,1032,128]{2,1,0:T(8,128)}, u32[]{:S(2)}, u32[]{:S(2)}) async-start(f32[8,1032,128]{2,1,0:T(8,128)} %pad_maximum_fusion), calls=%async_computation | async-start | bytes 8454144 | tf_op jit(solution)/shard_map/all_to_all | solution.py:288
  51.2 19.1 %collective-permute-start.1 = (f32[8192,128]{1,0:T(8,128)}, f32[8192,128]{1,0:T(8,128)}, u32[]{:S(2)}, u32[]{:S(2)}) collective-permute-start(f32[8192,128]{1,0:T(8,128)} %collective-permute-done.near_ref), channel_id=1, source_target_pairs={{0,1},{1,0},{2,3},{3,2},{4,5},{5,4},{6,7},{7,6},{8,9},{9,8},{10,11... | collective-permute-start | bytes 12582920 | tf_op jit(solution)/shard_map/ppermute | solution.py:283

commit v7 on v6

--- a/solution.py
+++ b/solution.py
@@ -21,7 +21,8 @@
 
 
 def product_kernel(
-    table_ref, own_ref, sent_ref, near_ref, far_ref, out_ref, gram_ref, tile_buf, vec_buf, tile_sem, vec_sem
+    count_ref, own_ref, sent_ref, near_ref, far_ref, out_ref, gram_ref,
+    count_buf, note_buf, tile_buf, vec_buf, count_sem, note_sem, tile_sem, vec_sem,
 ):
     slots = sent_ref.shape[0]
     size, width = tile_buf.shape[2:]
@@ -36,11 +37,19 @@
         start = pl.multiple_of(block * size, size)
         return pltpu.make_async_copy(source.at[pl.ds(start, size)], vec_buf.at[row, slot], vec_sem.at[row, slot])
 
+    counts = pltpu.make_async_copy(count_ref, count_buf, count_sem)
+    notes = pltpu.make_async_copy(sent_ref.at[:, pl.ds(rows_kept * size, 1)], note_buf, note_sem)
+    counts.start()
+    notes.start()
     copy_tiles(0).start()
-    kept_from, near_side = table_ref[slots + 1, 0] * rows_kept, table_ref[slots + 1, 1]
+    col = lax.axis_index("cols")
+    kept_from, near_side = col * rows_kept, 2 * (col % 2)
+    left_from = (lax.axis_index("rows") - 1) * blocks
+    counts.wait()
+    notes.wait()
 
     def count_of(row):
-        return table_ref[slots, kept_from + row]
+        return count_buf[kept_from + row]
 
     def fetch(row, carry):
         @pl.when(row > 0)
@@ -48,7 +57,7 @@
             copy_tiles(row).start()
 
         def fetch_vec(slot, inner):
-            block = table_ref[slot, kept_from + row]
+            block = note_buf[slot, 0, kept_from + row].astype(jnp.int32) - left_from
             side = (block >= blocks).astype(jnp.int32) + (block >= 2 * blocks).astype(jnp.int32)
             within = block - side * blocks
 
@@ -101,34 +110,23 @@
     gram_ref[...] = gram[:width, :width] + (gram[:width, width:] + gram[width:, :width]) + gram[width:, width:]
 
 
-def decode_kernel(first, count_ref, sent_ref, table_ref, note_buf, sem):
-    notes = pltpu.make_async_copy(sent_ref.at[:, pl.ds(first, SUBLANES)], note_buf, sem)
-    notes.start()
-    slots = note_buf.shape[0]
-    blocks = count_ref.shape[1]
-    row, col = lax.axis_index("rows"), lax.axis_index("cols")
-    table_ref[slots : slots + 1, :blocks] = count_ref[...]
-    at = lax.broadcasted_iota(jnp.int32, (1, table_ref.shape[1]), 1)
-    table_ref[slots + 1 : slots + 2, :] = jnp.where(at == 0, col, 2 * (col % 2))
-    notes.wait()
-    for slot in range(slots):
-        table_ref[slot : slot + 1, :] = note_buf[slot, 0:1, :].astype(jnp.int32) - (row - 1) * blocks
-
-
-def decode(counts, sent, first):
-    slots, _, size = sent.shape
+def hand_over_kernel(sent_ref, out_ref):
+    pass
+
+
+def hand_over(sent):
     return pl.pallas_call(
-        functools.partial(decode_kernel, first),
-        out_shape=jax.ShapeDtypeStruct((slots + SUBLANES, size), jnp.int32),
-        in_specs=[pl.BlockSpec(memory_space=pltpu.VMEM), pl.BlockSpec(memory_space=pl.ANY)],
-        out_specs=pl.BlockSpec(memory_space=pltpu.VMEM),
-        scratch_shapes=[pltpu.VMEM((slots, SUBLANES, size), jnp.float32), pltpu.SemaphoreType.DMA],
+        hand_over_kernel,
+        out_shape=jax.ShapeDtypeStruct(sent.shape, sent.dtype),
+        in_specs=[pl.BlockSpec(memory_space=pl.ANY)],
+        out_specs=pl.BlockSpec(memory_space=pl.ANY),
+        input_output_aliases={0: 0},
         compiler_params=pltpu.CompilerParams(vmem_limit_bytes=62 << 20),
         cost_estimate=pl.CostEstimate(flops=1 << 33, bytes_accessed=1 << 26, transcendentals=0),
-    )(counts, sent)
-
-
-def product_and_gram(table, own, sent, near, far, rows_kept, size):
+    )(sent)
+
+
+def product_and_gram(counts, own, sent, near, far, rows_kept, size):
     slots, width = sent.shape[0], own.shape[1]
     in_vmem = pl.BlockSpec(memory_space=pltpu.VMEM)
     anywhere = pl.BlockSpec(memory_space=pl.ANY)
@@ -138,27 +136,29 @@
             jax.ShapeDtypeStruct((rows_kept * size, width), jnp.float32),
             jax.ShapeDtypeStruct((width, width), jnp.float32),
         ),
-        in_specs=[pl.BlockSpec(memory_space=pltpu.SMEM)] + [anywhere] * 4,
+        in_specs=[anywhere] * 5,
         out_specs=(in_vmem, in_vmem),
         scratch_shapes=[
+            pltpu.SMEM(counts.shape, jnp.int32),
+            pltpu.SMEM((slots, 1, width), jnp.float32),
             pltpu.VMEM((rows_kept, slots, size, size), jnp.float32),
             pltpu.VMEM((rows_kept, slots, size, width), jnp.float32),
+            pltpu.SemaphoreType.DMA,
+            pltpu.SemaphoreType.DMA,
             pltpu.SemaphoreType.DMA((rows_kept,)),
             pltpu.SemaphoreType.DMA((rows_kept, slots)),
         ],
-        compiler_params=pltpu.CompilerParams(vmem_limit_bytes=62 << 20),
-    )(table, own, sent, near, far)
-
-
-def factor_kernel(nodes, gram_ref, rows_ref, basis_ref, factor_ref, rows_buf, basis_buf, rows_sem, basis_sem):
+        compiler_params=pltpu.CompilerParams(vmem_limit_bytes=50 << 20),
+    )(counts, own, sent, near, far)
+
+
+def factor_kernel(nodes, gram_ref, rows_ref, basis_ref, factor_ref, basis_buf, basis_sem):
     size = gram_ref.shape[0]
     groups = size // SUBLANES
     shape = (SUBLANES, size)
     lane = lax.broadcasted_iota(jnp.int32, shape, 1)
     sub = lax.broadcasted_iota(jnp.int32, shape, 0)
     root = jnp.sqrt(jnp.float32(nodes))
-    bring = pltpu.make_async_copy(rows_ref, rows_buf, rows_sem)
-    bring.start()
 
     def column(x, at):
         return jnp.broadcast_to(x[:, at : at + 1], shape)
@@ -209,13 +209,12 @@
             gram[below] = gram[below] - total([weights[i] * x_lines[i] for i in range(height)])
             inverse[below] = inverse[below] - total([weights[i] * v_lines[i] for i in range(height)])
     solver = jnp.concatenate(inverse, axis=0)
-    bring.wait()
-    chunk = rows_buf.shape[0] // CHUNKS
+    chunk = rows_ref.shape[0] // CHUNKS
     copies = []
     for at in range(CHUNKS):
         here = pl.ds(at * chunk, chunk)
         basis_buf[here, :] = lax.dot_general(
-            rows_buf[here, :], solver, (((1,), (1,)), ((), ())), precision=EXACT, preferred_element_type=jnp.float32
+            rows_ref[here, :], solver, (((1,), (1,)), ((), ())), precision=EXACT, preferred_element_type=jnp.float32
         )
         copies.append(pltpu.make_async_copy(basis_buf.at[here], basis_ref.at[here], basis_sem.at[at]))
         copies[-1].start()
@@ -225,17 +224,13 @@
 
 def basis_and_factor(nodes, gram, rows):
     in_vmem = pl.BlockSpec(memory_space=pltpu.VMEM)
-    in_hbm = pl.BlockSpec(memory_space=pltpu.HBM)
     return pl.pallas_call(
         functools.partial(factor_kernel, nodes),
         out_shape=(jax.ShapeDtypeStruct(rows.shape, jnp.float32), jax.ShapeDtypeStruct(gram.shape, jnp.float32)),
-        in_specs=[in_vmem, in_hbm],
-        out_specs=(in_hbm, in_vmem),
-        input_output_aliases={1: 0},
+        in_specs=[in_vmem, in_vmem],
+        out_specs=(pl.BlockSpec(memory_space=pl.ANY), in_vmem),
         scratch_shapes=[
             pltpu.VMEM(rows.shape, jnp.float32),
-            pltpu.VMEM(rows.shape, jnp.float32),
-            pltpu.SemaphoreType.DMA,
             pltpu.SemaphoreType.DMA((CHUNKS,)),
         ],
         compiler_params=pltpu.CompilerParams(vmem_limit_bytes=16 << 20),
@@ -286,8 +281,7 @@
     note = jnp.broadcast_to(note, (col_devices, SUBLANES, size))
     sent = jnp.concatenate([op_tiles.reshape(col_devices, rows_kept * size, size), note], axis=1)
     sent = lax.all_to_all(sent, "cols", 0, 0, tiled=True)
-    table = decode(live_counts.reshape(1, block_count), sent, rows_kept * size)
-    part_rows, gram = product_and_gram(table, block_vector, sent, near, far, rows_kept, size)
+    part_rows, gram = product_and_gram(live_counts, block_vector, hand_over(sent), near, far, rows_kept, size)
     gram = sum_over_devices(gram, row_devices, col_devices)
     return basis_and_factor(rows_here * row_devices, gram, part_rows)
 

time: 131 us -> 127 us (0.969)
  Pallas kernels: 14.6 us -> 11.5 us
    pallas_call x1, Pallas kernels: 2.02 us -> 0.01 us  [hand_over(): pl.pallas_call(hand_over_kernel, out_shape=jax.ShapeDtypeStruct(sent.shap...]
  transfers between devices with their start and end apart: 3 -> 3, of which waited for: 2 -> 2; matrix products, arithmetic and copies ran while one was open for 4% -> 4% of each run, Pallas kernels for 2% -> 0%
where the time goes in v7:
time: 127 us
  blocking collectives  47.2 us (37%)
  waiting for transfers between devices  42.7 us (34%)
  starting transfers between devices  19.8 us (16%)
  Pallas kernels  11.5 us (9%)
  other arithmetic  5.16 us (4%)
    all_to_all x3, blocking collectives, exchange(): lax.all_to_all(pieces, ('rows', 'cols'), 0, 0, axis_index_groups=groups,...  47.2 us
    ppermute x1, waiting for transfers between devices, on_device(): near = lax.ppermute(block_vector, ('rows', 'cols'), steps)  32.1 us
    all_to_all x1, waiting for transfers between devices, on_device(): sent = lax.all_to_all(sent, 'cols', 0, 0, tiled=True)  10.6 us
    ppermute x1, starting transfers between devices, on_device(): near = lax.ppermute(block_vector, ('rows', 'cols'), steps)  8.79 us
    ppermute x1, starting transfers between devices, on_device(): far = lax.ppermute(near, 'cols', [(i, i ^ 1) for i in range(col_devices)])  6.49 us
    pallas_call x1, Pallas kernels, basis_and_factor(): pl.pallas_call(functools.partial(factor_kernel, nodes), out_shape=(jax.Sh...  5.82 us
    pallas_call x1, Pallas kernels, product_and_gram(): pl.pallas_call(product_kernel, out_shape=(jax.ShapeDtypeStruct((rows_kept...  5.67 us
    all_to_all x1, starting transfers between devices, on_device(): sent = lax.all_to_all(sent, 'cols', 0, 0, tiled=True)  4.51 us
  transfers between devices with their start and end apart: 3, of which 2 were waited for; matrix products, arithmetic and copies ran while one was open for 4% of the time, Pallas kernels for 0%

profile of v7, /device:TPU:1, one launch (start us, length us, event | category | flops | bytes accessed | tf_op | source)
XLA Modules:
  0.0 127.1 jit_solution(2218248113939129015)
XLA Ops:
  0.6 8.8 %collective-permute-start = (f32[8192,128]{1,0:T(8,128)}, f32[8192,128]{1,0:T(8,128)}, u32[]{:S(2)}, u32[]{:S(2)}) collective-permute-start(f32[8192,128]{1,0:T(8,128)} %own_ref.1), channel_id=1, source_target_pairs={{0,8},{1,0},{2,10},{3,2},{4,12},{5,4},{6,14},{7,6},{8,16},{9,1},{1... | collective-permute-start | bytes 12582920 | tf_op jit(solution)/shard_map/ppermute | solution.py:277
  9.4 0.7 convert_bitcast_fusion
  10.1 4.4 %pad_maximum_fusion = f32[8,1032,128]{2,1,0:T(8,128)} fusion(f32[8,8,128]{2,1,0:T(8,128)S(1)} %broadcast_in_dim.9, f32[8,1024,128]{2,1,0:T(8,128)} %bitcast.9), kind=kLoop, calls=%fused_computation | loop fusion | flops 1056768 | bytes 8454144 | tf_op jit(solution)/shard_map/concatenate | solution.py:282
  14.5 4.5 %all-to-all-start = ((f32[8,1032,128]{2,1,0:T(8,128)}), f32[8,1032,128]{2,1,0:T(8,128)}, u32[]{:S(2)}, u32[]{:S(2)}) async-start(f32[8,1032,128]{2,1,0:T(8,128)} %pad_maximum_fusion), calls=%async_computation | async-start | bytes 8454144 | tf_op jit(solution)/shard_map/all_to_all | solution.py:283
  19.1 0.0 copy-start
  19.1 32.1 %collective-permute-done.near_ref = f32[8192,128]{1,0:T(8,128)} collective-permute-done((f32[8192,128]{1,0:T(8,128)}, f32[8192,128]{1,0:T(8,128)}, u32[]{:S(2)}, u32[]{:S(2)}) %collective-permute-start) | collective-permute-done | bytes 4194336 | tf_op jit(solution)/shard_map/ppermute | solution.py:277
  51.2 6.5 %collective-permute-start.1 = (f32[8192,128]{1,0:T(8,128)}, f32[8192,128]{1,0:T(8,128)}, u32[]{:S(2)}, u32[]{:S(2)}) collective-permute-start(f32[8192,128]{1,0:T(8,128)} %collective-permute-done.near_ref), channel_id=1, source_target_pairs={{0,1},{1,0},{2,3},{3,2},{4,5},{5,4},{6,7},{7,6},{8,9},{9,8},{10,11... | collective-permute-start | bytes 12582920 | tf_op jit(solution)/shard_map/ppermute | solution.py:278
  57.7 10.6 %all-to-all-done.sent_ref = f32[8,1032,128]{2,1,0:T(8,128)} async-done(((f32[8,1032,128]{2,1,0:T(8,128)}), f32[8,1032,128]{2,1,0:T(8,128)}, u32[]{:S(2)}, u32[]{:S(2)}) %all-to-all-start) | async-done | bytes 4227104 | tf_op jit(solution)/shard_map/all_to_all | solution.py:283
  68.2 0.0 collective-permute-done.1.far_ref
  68.2 0.0 copy-done
  68.2 5.7 %shard_map.60 = (f32[1024,128]{1,0:T(8,128)S(1)}, f32[128,128]{1,0:T(8,128)S(1)}) custom-call(s32[64]{0:T(128)S(1)} %copy-done, f32[8192,128]{1,0:T(8,128)} %own_ref.1, f32[8,1032,128]{2,1,0:T(8,128)} %shard_map.59.sent_ref, f32[8192,128]{1,0:T(8,128)} %collective-permute-done.near_ref, f32[8192,128]{1,0:T(8,128)} %collective-permute-done.1.far_ref), custom_call_target="tpu_custom_call" | custom-call | tf_op jit(solution)/shard_map/pallas_call | solution.py:133
  73.9 11.2 %all_to_all.20 = f32[32,4,128]{2,1,0:T(4,128)S(1)} all-to-all(f32[32,4,128]{2,1,0:T(4,128)S(1)} %bitcast.8), channel_id=1, replica_groups={{0,1,2,3,4,5,6,7,8,9,10,11,12,13,14,15,16,17,18,19,20,21,22,23,24,25,26..., dimensions={0} | all-to-all | bytes 131072 | tf_op jit(solution)/shard_map/all_to_all | solution.py:248
  85.1 23.8 %all_to_all.21 = f32[16,4,128]{2,1,0:T(4,128)S(1)} all-to-all(f32[16,4,128]{2,1,0:T(4,128)S(1)} %broadcast_in_dim.10), channel_id=1, replica_groups={{0,32,64,96,128,160,192,224,256,288,320,352,384,416,448,480},{1,33,65,9..., dimensions={0} | all-to-all | bytes 65536 | tf_op jit(solution)/shard_map/all_to_all | solution.py:248
  109.0 12.3 %all_to_all.22 = f32[32,4,128]{2,1,0:T(4,128)S(1)} all-to-all(f32[32,4,128]{2,1,0:T(4,128)S(1)} %broadcast_in_dim.22), channel_id=1, replica_groups={{0,1,2,3,4,5,6,7,8,9,10,11,12,13,14,15,16,17,18,19,20,21,22,23,24,25,26..., dimensions={0} | all-to-all | bytes 131072 | tf_op jit(solution)/shard_map/all_to_all | solution.py:248
  121.2 5.8 %shard_map.61 = (f32[1024,128]{1,0:T(8,128)}, f32[128,128]{1,0:T(8,128)}) custom-call(f32[128,128]{1,0:T(8,128)S(1)} %bitcast.7, f32[1024,128]{1,0:T(8,128)S(1)} %get-tuple-element.5.rows_ref), custom_call_target="tpu_custom_call" | custom-call | tf_op jit(solution)/shard_map/pallas_call | solution.py:227
  (7 shorter events, 0.1 us)
Async XLA Ops:
  0.6 50.5 %collective-permute-start = (f32[8192,128]{1,0:T(8,128)}, f32[8192,128]{1,0:T(8,128)}, u32[]{:S(2)}, u32[]{:S(2)}) collective-permute-start(f32[8192,128]{1,0:T(8,128)} %own_ref.1), channel_id=1, source_target_pairs={{0,8},{1,0},{2,10},{3,2},{4,12},{5,4},{6,14},{7,6},{8,16},{9,1},{1... | collective-permute-start | bytes 12582920 | tf_op jit(solution)/shard_map/ppermute | solution.py:277
  14.5 53.7 %all-to-all-start = ((f32[8,1032,128]{2,1,0:T(8,128)}), f32[8,1032,128]{2,1,0:T(8,128)}, u32[]{:S(2)}, u32[]{:S(2)}) async-start(f32[8,1032,128]{2,1,0:T(8,128)} %pad_maximum_fusion), calls=%async_computation | async-start | bytes 8454144 | tf_op jit(solution)/shard_map/all_to_all | solution.py:283
  19.1 49.2 %copy-start = (s32[64]{0:T(128)S(1)}, s32[64]{0:T(128)}, u32[]{:S(2)}) copy-start(s32[64]{0:T(128)} %count_ref.1) | copy-start | bytes 772
  51.2 17.1 %collective-permute-start.1 = (f32[8192,128]{1,0:T(8,128)}, f32[8192,128]{1,0:T(8,128)}, u32[]{:S(2)}, u32[]{:S(2)}) collective-permute-start(f32[8192,128]{1,0:T(8,128)} %collective-permute-done.near_ref), channel_id=1, source_target_pairs={{0,1},{1,0},{2,3},{3,2},{4,5},{5,4},{6,7},{7,6},{8,9},{9,8},{10,11... | collective-permute-start | bytes 12582920 | tf_op jit(solution)/shard_map/ppermute | solution.py:278

commit v8 on v7

--- a/solution.py
+++ b/solution.py
@@ -274,12 +274,12 @@
     for r, c in itertools.product(range(row_devices), range(col_devices)):
         to_r, to_c = fetched_by(r, c)
         steps.append((r * col_devices + c, to_r * col_devices + to_c))
-    near = lax.ppermute(block_vector, ("rows", "cols"), steps)
-    far = lax.ppermute(near, "cols", [(i, i ^ 1) for i in range(col_devices)])
-
     note = jnp.pad(tile_cols.reshape(1, 1, block_count).astype(jnp.float32), ((0, 0), (0, 0), (0, size - block_count)))
     note = jnp.broadcast_to(note, (col_devices, SUBLANES, size))
     sent = jnp.concatenate([op_tiles.reshape(col_devices, rows_kept * size, size), note], axis=1)
+    source, sent = lax.optimization_barrier((block_vector, sent))
+    near = lax.ppermute(source, ("rows", "cols"), steps)
+    far = lax.ppermute(near, "cols", [(i, i ^ 1) for i in range(col_devices)])
     sent = lax.all_to_all(sent, "cols", 0, 0, tiled=True)
     part_rows, gram = product_and_gram(live_counts, block_vector, hand_over(sent), near, far, rows_kept, size)
     gram = sum_over_devices(gram, row_devices, col_devices)

time: 127 us -> 132 us (1.039)
  blocking collectives: 47.2 us -> 50.7 us
  waiting for transfers between devices: 42.7 us -> 44.3 us
    all_to_all x1, waiting for transfers between devices: 10.6 us -> 5.49 us  [on_device(): sent = lax.all_to_all(sent, 'cols', 0, 0, tiled=True)]
    ppermute x1, waiting for transfers between devices: 32.1 us -> 37.2 us  [on_device(): near = lax.ppermute(source, ('rows', 'cols'), steps)]
    all_to_all x3, blocking collectives: 47.2 us -> 50.7 us  [exchange(): lax.all_to_all(pieces, ('rows', 'cols'), 0, 0, axis_index_groups=groups,...]
    ppermute x1, waiting for transfers between devices: 0.01 us -> 1.62 us  [on_device(): far = lax.ppermute(near, 'cols', [(i, i ^ 1) for i in range(col_devices)])]
  transfers between devices with their start and end apart: 3 -> 3, of which waited for: 2 -> 3; matrix products, arithmetic and copies ran while one was open for 4% -> 0% of each run, Pallas kernels for 0% -> 0%
where the time goes in v8:
time: 132 us
  blocking collectives  50.7 us (38%)
  waiting for transfers between devices  44.3 us (34%)
  starting transfers between devices  19.8 us (15%)
  Pallas kernels  11.2 us (8%)
  other arithmetic  5.16 us (4%)
    all_to_all x3, blocking collectives, exchange(): lax.all_to_all(pieces, ('rows', 'cols'), 0, 0, axis_index_groups=groups,...  50.7 us
    ppermute x1, waiting for transfers between devices, on_device(): near = lax.ppermute(source, ('rows', 'cols'), steps)  37.2 us
    ppermute x1, starting transfers between devices, on_device(): near = lax.ppermute(source, ('rows', 'cols'), steps)  8.78 us
    ppermute x1, starting transfers between devices, on_device(): far = lax.ppermute(near, 'cols', [(i, i ^ 1) for i in range(col_devices)])  6.49 us
    pallas_call x1, Pallas kernels, basis_and_factor(): pl.pallas_call(functools.partial(factor_kernel, nodes), out_shape=(jax.Sh...  5.82 us
    all_to_all x1, waiting for transfers between devices, on_device(): sent = lax.all_to_all(sent, 'cols', 0, 0, tiled=True)  5.49 us
    pallas_call x1, Pallas kernels, product_and_gram(): pl.pallas_call(product_kernel, out_shape=(jax.ShapeDtypeStruct((rows_kept...  5.36 us
    all_to_all x1, starting transfers between devices, on_device(): sent = lax.all_to_all(sent, 'cols', 0, 0, tiled=True)  4.52 us
  transfers between devices with their start and end apart: 3, of which 3 were waited for; matrix products, arithmetic and copies ran while one was open for 0% of the time, Pallas kernels for 0%

profile of v8, /device:TPU:1, one launch (start us, length us, event | category | flops | bytes accessed | tf_op | source)
XLA Modules:
  0.0 131.9 jit_solution(10018408190164081620)
XLA Ops:
  0.6 0.7 convert_bitcast_fusion
  1.3 4.4 %pad_maximum_fusion = f32[8,1032,128]{2,1,0:T(8,128)} fusion(f32[8,8,128]{2,1,0:T(8,128)S(1)} %broadcast_in_dim.9, f32[8,1024,128]{2,1,0:T(8,128)} %bitcast.9), kind=kLoop, calls=%fused_computation | loop fusion | flops 1056768 | bytes 8454144 | tf_op jit(solution)/shard_map/concatenate | solution.py:279
  5.7 8.8 %collective-permute-start = (f32[8192,128]{1,0:T(8,128)}, f32[8192,128]{1,0:T(8,128)}, u32[]{:S(2)}, u32[]{:S(2)}) collective-permute-start(f32[8192,128]{1,0:T(8,128)} %own_ref.1), channel_id=1, source_target_pairs={{0,8},{1,0},{2,10},{3,2},{4,12},{5,4},{6,14},{7,6},{8,16},{9,1},{1... | collective-permute-start | bytes 12582920 | tf_op jit(solution)/shard_map/ppermute | solution.py:281
  14.5 4.5 %all-to-all-start = ((f32[8,1032,128]{2,1,0:T(8,128)}), f32[8,1032,128]{2,1,0:T(8,128)}, u32[]{:S(2)}, u32[]{:S(2)}) async-start(f32[8,1032,128]{2,1,0:T(8,128)} %pad_maximum_fusion), calls=%async_computation | async-start | bytes 8454144 | tf_op jit(solution)/shard_map/all_to_all | solution.py:283
  19.1 0.0 copy-start
  19.1 37.2 %collective-permute-done.near_ref = f32[8192,128]{1,0:T(8,128)} collective-permute-done((f32[8192,128]{1,0:T(8,128)}, f32[8192,128]{1,0:T(8,128)}, u32[]{:S(2)}, u32[]{:S(2)}) %collective-permute-start) | collective-permute-done | bytes 4194336 | tf_op jit(solution)/shard_map/ppermute | solution.py:281
  56.3 6.5 %collective-permute-start.1 = (f32[8192,128]{1,0:T(8,128)}, f32[8192,128]{1,0:T(8,128)}, u32[]{:S(2)}, u32[]{:S(2)}) collective-permute-start(f32[8192,128]{1,0:T(8,128)} %collective-permute-done.near_ref), channel_id=1, source_target_pairs={{0,1},{1,0},{2,3},{3,2},{4,5},{5,4},{6,7},{7,6},{8,9},{9,8},{10,11... | collective-permute-start | bytes 12582920 | tf_op jit(solution)/shard_map/ppermute | solution.py:282
  62.8 5.5 %all-to-all-done.sent_ref = f32[8,1032,128]{2,1,0:T(8,128)} async-done(((f32[8,1032,128]{2,1,0:T(8,128)}), f32[8,1032,128]{2,1,0:T(8,128)}, u32[]{:S(2)}, u32[]{:S(2)}) %all-to-all-start) | async-done | bytes 4227104 | tf_op jit(solution)/shard_map/all_to_all | solution.py:283
  68.2 1.6 %collective-permute-done.1.far_ref = f32[8192,128]{1,0:T(8,128)} collective-permute-done((f32[8192,128]{1,0:T(8,128)}, f32[8192,128]{1,0:T(8,128)}, u32[]{:S(2)}, u32[]{:S(2)}) %collective-permute-start.1) | collective-permute-done | bytes 4194336 | tf_op jit(solution)/shard_map/ppermute | solution.py:282
  69.9 0.0 copy-done
  69.9 5.4 %shard_map.60 = (f32[1024,128]{1,0:T(8,128)S(1)}, f32[128,128]{1,0:T(8,128)S(1)}) custom-call(s32[64]{0:T(128)S(1)} %copy-done, f32[8192,128]{1,0:T(8,128)} %own_ref.1, f32[8,1032,128]{2,1,0:T(8,128)} %shard_map.59.sent_ref, f32[8192,128]{1,0:T(8,128)} %collective-permute-done.near_ref, f32[8192,128]{1,0:T(8,128)} %collective-permute-done.1.far_ref), custom_call_target="tpu_custom_call" | custom-call | tf_op jit(solution)/shard_map/pallas_call | solution.py:133
  75.2 12.1 %all_to_all.20 = f32[32,4,128]{2,1,0:T(4,128)S(1)} all-to-all(f32[32,4,128]{2,1,0:T(4,128)S(1)} %bitcast.8), channel_id=1, replica_groups={{0,1,2,3,4,5,6,7,8,9,10,11,12,13,14,15,16,17,18,19,20,21,22,23,24,25,26..., dimensions={0} | all-to-all | bytes 131072 | tf_op jit(solution)/shard_map/all_to_all | solution.py:248
  87.4 26.4 %all_to_all.21 = f32[16,4,128]{2,1,0:T(4,128)S(1)} all-to-all(f32[16,4,128]{2,1,0:T(4,128)S(1)} %broadcast_in_dim.10), channel_id=1, replica_groups={{0,32,64,96,128,160,192,224,256,288,320,352,384,416,448,480},{1,33,65,9..., dimensions={0} | all-to-all | bytes 65536 | tf_op jit(solution)/shard_map/all_to_all | solution.py:248
  113.8 12.3 %all_to_all.22 = f32[32,4,128]{2,1,0:T(4,128)S(1)} all-to-all(f32[32,4,128]{2,1,0:T(4,128)S(1)} %broadcast_in_dim.22), channel_id=1, replica_groups={{0,1,2,3,4,5,6,7,8,9,10,11,12,13,14,15,16,17,18,19,20,21,22,23,24,25,26..., dimensions={0} | all-to-all | bytes 131072 | tf_op jit(solution)/shard_map/all_to_all | solution.py:248
  126.1 5.8 %shard_map.61 = (f32[1024,128]{1,0:T(8,128)}, f32[128,128]{1,0:T(8,128)}) custom-call(f32[128,128]{1,0:T(8,128)S(1)} %bitcast.7, f32[1024,128]{1,0:T(8,128)S(1)} %get-tuple-element.9.rows_ref), custom_call_target="tpu_custom_call" | custom-call | tf_op jit(solution)/shard_map/pallas_call | solution.py:227
  (7 shorter events, 0.1 us)
Async XLA Ops:
  5.7 50.5 %collective-permute-start = (f32[8192,128]{1,0:T(8,128)}, f32[8192,128]{1,0:T(8,128)}, u32[]{:S(2)}, u32[]{:S(2)}) collective-permute-start(f32[8192,128]{1,0:T(8,128)} %own_ref.1), channel_id=1, source_target_pairs={{0,8},{1,0},{2,10},{3,2},{4,12},{5,4},{6,14},{7,6},{8,16},{9,1},{1... | collective-permute-start | bytes 12582920 | tf_op jit(solution)/shard_map/ppermute | solution.py:281
  14.5 53.7 %all-to-all-start = ((f32[8,1032,128]{2,1,0:T(8,128)}), f32[8,1032,128]{2,1,0:T(8,128)}, u32[]{:S(2)}, u32[]{:S(2)}) async-start(f32[8,1032,128]{2,1,0:T(8,128)} %pad_maximum_fusion), calls=%async_computation | async-start | bytes 8454144 | tf_op jit(solution)/shard_map/all_to_all | solution.py:283
  19.1 50.8 %copy-start = (s32[64]{0:T(128)S(1)}, s32[64]{0:T(128)}, u32[]{:S(2)}) copy-start(s32[64]{0:T(128)} %count_ref.1) | copy-start | bytes 772
  56.3 13.6 %collective-permute-start.1 = (f32[8192,128]{1,0:T(8,128)}, f32[8192,128]{1,0:T(8,128)}, u32[]{:S(2)}, u32[]{:S(2)}) collective-permute-start(f32[8192,128]{1,0:T(8,128)} %collective-permute-done.near_ref), channel_id=1, source_target_pairs={{0,1},{1,0},{2,3},{3,2},{4,5},{5,4},{6,7},{7,6},{8,9},{9,8},{10,11... | collective-permute-start | bytes 12582920 | tf_op jit(solution)/shard_map/ppermute | solution.py:282

commit v9 on v7

--- a/solution.py
+++ b/solution.py
@@ -108,6 +108,46 @@
     both = jnp.concatenate([high, low], axis=1)
     gram = lax.dot_general(both, both, (((0,), (0,)), ((), ())), preferred_element_type=jnp.float32)
     gram_ref[...] = gram[:width, :width] + (gram[:width, width:] + gram[width:, :width]) + gram[width:, width:]
+
+
+def pack_kernel(tile_ref, number_ref, out_ref, tile_buf, note_buf, in_sem, out_sem, note_sem):
+    slots, rows, _ = tile_ref.shape
+    arrive = [pltpu.make_async_copy(tile_ref.at[at], tile_buf.at[at], in_sem.at[at]) for at in range(slots)]
+    leave = [
+        pltpu.make_async_copy(tile_buf.at[at], out_ref.at[at, pl.ds(0, rows)], out_sem.at[at]) for at in range(slots)
+    ]
+    for copy in arrive:
+        copy.start()
+    blocks = number_ref.shape[1]
+    note_buf[...] = jnp.zeros_like(note_buf)
+    note_buf[:, :, :blocks] = jnp.broadcast_to(number_ref[...].astype(jnp.float32)[None], (slots, SUBLANES, blocks))
+    note = pltpu.make_async_copy(note_buf, out_ref.at[:, pl.ds(rows, SUBLANES)], note_sem)
+    note.start()
+    for at in range(slots):
+        arrive[at].wait()
+        leave[at].start()
+    for copy in leave:
+        copy.wait()
+    note.wait()
+
+
+def pack(tiles, numbers):
+    slots, rows, size = tiles.shape
+    return pl.pallas_call(
+        pack_kernel,
+        out_shape=jax.ShapeDtypeStruct((slots, rows + SUBLANES, size), jnp.float32),
+        in_specs=[pl.BlockSpec(memory_space=pl.ANY), pl.BlockSpec(memory_space=pltpu.VMEM)],
+        out_specs=pl.BlockSpec(memory_space=pl.ANY),
+        scratch_shapes=[
+            pltpu.VMEM(tiles.shape, jnp.float32),
+            pltpu.VMEM((slots, SUBLANES, size), jnp.float32),
+            pltpu.SemaphoreType.DMA((slots,)),
+            pltpu.SemaphoreType.DMA((slots,)),
+            pltpu.SemaphoreType.DMA,
+        ],
+        compiler_params=pltpu.CompilerParams(vmem_limit_bytes=62 << 20),
+        cost_estimate=pl.CostEstimate(flops=0, bytes_accessed=8 << 20, transcendentals=0),
+    )(tiles, numbers)
 
 
 def hand_over_kernel(sent_ref, out_ref):
@@ -277,9 +317,7 @@
     near = lax.ppermute(block_vector, ("rows", "cols"), steps)
     far = lax.ppermute(near, "cols", [(i, i ^ 1) for i in range(col_devices)])
 
-    note = jnp.pad(tile_cols.reshape(1, 1, block_count).astype(jnp.float32), ((0, 0), (0, 0), (0, size - block_count)))
-    note = jnp.broadcast_to(note, (col_devices, SUBLANES, size))
-    sent = jnp.concatenate([op_tiles.reshape(col_devices, rows_kept * size, size), note], axis=1)
+    sent = pack(op_tiles.reshape(col_devices, rows_kept * size, size), tile_cols.reshape(1, block_count))
     sent = lax.all_to_all(sent, "cols", 0, 0, tiled=True)
     part_rows, gram = product_and_gram(live_counts, block_vector, hand_over(sent), near, far, rows_kept, size)
     gram = sum_over_devices(gram, row_devices, col_devices)

time: 127 us -> 127 us (level)
  other arithmetic: 5.16 us -> 0.07 us
  Pallas kernels: 11.5 us -> 15.6 us
    concatenate x1 -> x0, other arithmetic: 4.43 us -> none  [on_device(): jnp.concatenate([op_tiles.reshape(col_devices, rows_kept * size, size), n...]
    pallas_call x0 -> x1, Pallas kernels: none -> 4.29 us  [pack(): pl.pallas_call(pack_kernel, out_shape=jax.ShapeDtypeStruct((slots, rows +...]
  transfers between devices with their start and end apart: 3 -> 3, of which waited for: 2 -> 2; matrix products, arithmetic and copies ran while one was open for 4% -> 0% of each run, Pallas kernels for 0% -> 3%
where the time goes in v9:
time: 127 us
  blocking collectives  48.3 us (38%)
  waiting for transfers between devices  42.7 us (34%)
  starting transfers between devices  19.8 us (16%)
  Pallas kernels  15.6 us (12%)
    all_to_all x3, blocking collectives, exchange(): lax.all_to_all(pieces, ('rows', 'cols'), 0, 0, axis_index_groups=groups,...  48.3 us
    ppermute x1, waiting for transfers between devices, on_device(): near = lax.ppermute(block_vector, ('rows', 'cols'), steps)  32.9 us
    all_to_all x1, waiting for transfers between devices, on_device(): sent = lax.all_to_all(sent, 'cols', 0, 0, tiled=True)  9.79 us
    ppermute x1, starting transfers between devices, on_device(): near = lax.ppermute(block_vector, ('rows', 'cols'), steps)  8.79 us
    ppermute x1, starting transfers between devices, on_device(): far = lax.ppermute(near, 'cols', [(i, i ^ 1) for i in range(col_devices)])  6.49 us
    pallas_call x1, Pallas kernels, basis_and_factor(): pl.pallas_call(functools.partial(factor_kernel, nodes), out_shape=(jax.Sh...  5.81 us
    pallas_call x1, Pallas kernels, product_and_gram(): pl.pallas_call(product_kernel, out_shape=(jax.ShapeDtypeStruct((rows_kept...  5.51 us
    all_to_all x1, starting transfers between devices, on_device(): sent = lax.all_to_all(sent, 'cols', 0, 0, tiled=True)  4.52 us
  transfers between devices with their start and end apart: 3, of which 2 were waited for; matrix products, arithmetic and copies ran while one was open for 0% of the time, Pallas kernels for 3%

profile of v9, /device:TPU:1, one launch (start us, length us, event | category | flops | bytes accessed | tf_op | source)
XLA Modules:
  0.0 127.1 jit_solution(14290910224874253483)
XLA Ops:
  0.6 8.8 %collective-permute-start = (f32[8192,128]{1,0:T(8,128)}, f32[8192,128]{1,0:T(8,128)}, u32[]{:S(2)}, u32[]{:S(2)}) collective-permute-start(f32[8192,128]{1,0:T(8,128)} %own_ref.1), channel_id=1, source_target_pairs={{0,8},{1,0},{2,10},{3,2},{4,12},{5,4},{6,14},{7,6},{8,16},{9,1},{1... | collective-permute-start | bytes 12582920 | tf_op jit(solution)/shard_map/ppermute | solution.py:317
  9.4 4.3 %shard_map.59 = f32[8,1032,128]{2,1,0:T(8,128)} custom-call(f32[8,1024,128]{2,1,0:T(8,128)} %bitcast.6, s32[1,64]{1,0:T(1,128)} %bitcast.7), custom_call_target="tpu_custom_call" | custom-call | bytes 8388608 | tf_op jit(solution)/shard_map/pallas_call | solution.py:136
  13.7 4.5 %all-to-all-start = ((f32[8,1032,128]{2,1,0:T(8,128)}), f32[8,1032,128]{2,1,0:T(8,128)}, u32[]{:S(2)}, u32[]{:S(2)}) async-start(f32[8,1032,128]{2,1,0:T(8,128)} %shard_map.59), calls=%async_computation | async-start | bytes 8454144 | tf_op jit(solution)/shard_map/all_to_all | solution.py:321
  18.3 0.0 copy-start
  18.3 32.9 %collective-permute-done.near_ref = f32[8192,128]{1,0:T(8,128)} collective-permute-done((f32[8192,128]{1,0:T(8,128)}, f32[8192,128]{1,0:T(8,128)}, u32[]{:S(2)}, u32[]{:S(2)}) %collective-permute-start) | collective-permute-done | bytes 4194336 | tf_op jit(solution)/shard_map/ppermute | solution.py:317
  51.2 6.5 %collective-permute-start.1 = (f32[8192,128]{1,0:T(8,128)}, f32[8192,128]{1,0:T(8,128)}, u32[]{:S(2)}, u32[]{:S(2)}) collective-permute-start(f32[8192,128]{1,0:T(8,128)} %collective-permute-done.near_ref), channel_id=1, source_target_pairs={{0,1},{1,0},{2,3},{3,2},{4,5},{5,4},{6,7},{7,6},{8,9},{9,8},{10,11... | collective-permute-start | bytes 12582920 | tf_op jit(solution)/shard_map/ppermute | solution.py:318
  57.7 9.8 %all-to-all-done.sent_ref = f32[8,1032,128]{2,1,0:T(8,128)} async-done(((f32[8,1032,128]{2,1,0:T(8,128)}), f32[8,1032,128]{2,1,0:T(8,128)}, u32[]{:S(2)}, u32[]{:S(2)}) %all-to-all-start) | async-done | bytes 4227104 | tf_op jit(solution)/shard_map/all_to_all | solution.py:321
  67.5 0.0 collective-permute-done.1.far_ref
  67.5 0.0 copy-done
  67.5 5.5 %shard_map.61 = (f32[1024,128]{1,0:T(8,128)S(1)}, f32[128,128]{1,0:T(8,128)S(1)}) custom-call(s32[64]{0:T(128)S(1)} %copy-done, f32[8192,128]{1,0:T(8,128)} %own_ref.1, f32[8,1032,128]{2,1,0:T(8,128)} %shard_map.60.sent_ref, f32[8192,128]{1,0:T(8,128)} %collective-permute-done.near_ref, f32[8192,128]{1,0:T(8,128)} %collective-permute-done.1.far_ref), custom_call_target="tpu_custom_call" | custom-call | tf_op jit(solution)/shard_map/pallas_call | solution.py:173
  73.0 11.1 %all_to_all.20 = f32[32,4,128]{2,1,0:T(4,128)S(1)} all-to-all(f32[32,4,128]{2,1,0:T(4,128)S(1)} %bitcast.5), channel_id=1, replica_groups={{0,1,2,3,4,5,6,7,8,9,10,11,12,13,14,15,16,17,18,19,20,21,22,23,24,25,26..., dimensions={0} | all-to-all | bytes 131072 | tf_op jit(solution)/shard_map/all_to_all | solution.py:288
  84.2 24.8 %all_to_all.21 = f32[16,4,128]{2,1,0:T(4,128)S(1)} all-to-all(f32[16,4,128]{2,1,0:T(4,128)S(1)} %broadcast_in_dim.4), channel_id=1, replica_groups={{0,32,64,96,128,160,192,224,256,288,320,352,384,416,448,480},{1,33,65,9..., dimensions={0} | all-to-all | bytes 65536 | tf_op jit(solution)/shard_map/all_to_all | solution.py:288
  109.0 12.3 %all_to_all.22 = f32[32,4,128]{2,1,0:T(4,128)S(1)} all-to-all(f32[32,4,128]{2,1,0:T(4,128)S(1)} %broadcast_in_dim.5), channel_id=1, replica_groups={{0,1,2,3,4,5,6,7,8,9,10,11,12,13,14,15,16,17,18,19,20,21,22,23,24,25,26..., dimensions={0} | all-to-all | bytes 131072 | tf_op jit(solution)/shard_map/all_to_all | solution.py:288
  121.3 5.8 %shard_map.62 = (f32[1024,128]{1,0:T(8,128)}, f32[128,128]{1,0:T(8,128)}) custom-call(f32[128,128]{1,0:T(8,128)S(1)} %bitcast.4, f32[1024,128]{1,0:T(8,128)S(1)} %get-tuple-element.5.rows_ref), custom_call_target="tpu_custom_call" | custom-call | tf_op jit(solution)/shard_map/pallas_call | solution.py:267
  (5 shorter events, 0.1 us)
Async XLA Ops:
  0.6 50.5 %collective-permute-start = (f32[8192,128]{1,0:T(8,128)}, f32[8192,128]{1,0:T(8,128)}, u32[]{:S(2)}, u32[]{:S(2)}) collective-permute-start(f32[8192,128]{1,0:T(8,128)} %own_ref.1), channel_id=1, source_target_pairs={{0,8},{1,0},{2,10},{3,2},{4,12},{5,4},{6,14},{7,6},{8,16},{9,1},{1... | collective-permute-start | bytes 12582920 | tf_op jit(solution)/shard_map/ppermute | solution.py:317
  13.7 53.7 %all-to-all-start = ((f32[8,1032,128]{2,1,0:T(8,128)}), f32[8,1032,128]{2,1,0:T(8,128)}, u32[]{:S(2)}, u32[]{:S(2)}) async-start(f32[8,1032,128]{2,1,0:T(8,128)} %shard_map.59), calls=%async_computation | async-start | bytes 8454144 | tf_op jit(solution)/shard_map/all_to_all | solution.py:321
  18.3 49.2 %copy-start = (s32[64]{0:T(128)S(1)}, s32[64]{0:T(128)}, u32[]{:S(2)}) copy-start(s32[64]{0:T(128)} %count_ref.1) | copy-start | bytes 772
  51.2 16.3 %collective-permute-start.1 = (f32[8192,128]{1,0:T(8,128)}, f32[8192,128]{1,0:T(8,128)}, u32[]{:S(2)}, u32[]{:S(2)}) collective-permute-start(f32[8192,128]{1,0:T(8,128)} %collective-permute-done.near_ref), channel_id=1, source_target_pairs={{0,1},{1,0},{2,3},{3,2},{4,5},{5,4},{6,7},{7,6},{8,9},{9,8},{10,11... | collective-permute-start | bytes 12582920 | tf_op jit(solution)/shard_map/ppermute | solution.py:318
